TPU v7x, 256 devices: a whole 4x4x8 slice. The times are simulated.
256 devices in a mesh: fsdp: 8 (over y, core), tp: 8 (over z), rep: 4 (over x).
Axes of the slice: x: 4, y: 4, z: 8, core: 2. Of those that a mesh axis runs over, the one named last changes fastest.
Arguments:
- train_inputs: bfloat16 [20480, 8192], P(('fsdp', 'rep'), 'tp'), may hold values from -6 to 6
- kv_grads: bfloat16 [20480, 2048], P(('fsdp', 'rep'), 'tp'), may hold values from -0.125 to 0.125
- master: float32 [8192, 2048], P(('fsdp', 'rep'), 'tp'), may hold values from -0.0234375 to 0.0234375
- first_moment: bfloat16 [8192, 2048], P(('fsdp', 'rep'), 'tp'), may hold values from -0.29882812 to 0.29882812
- second_moment: bfloat16 [8192, 2048], P(('fsdp', 'rep'), 'tp'), may hold values from 0.019897461 to 0.31835938
- hidden_states: bfloat16 [4, 1024, 8192], P(None, ('fsdp', 'rep')), may hold values from -18 to 18
- queries: bfloat16 [4, 1024, 8192], P(None, ('fsdp', 'rep'), 'tp'), may hold values from -24 to 24
- kv_cache: bfloat16 [1024, 256, 2048], P(('fsdp', 'rep'), None, 'tp'), may hold values from -24 to 24
- cache_lengths: int32 [1024], P(('fsdp', 'rep')), may hold values from 2 to 256, as said below
Outputs:
- new_master: float32 [8192, 2048], P(('fsdp', 'rep'), 'tp')
- new_first: bfloat16 [8192, 2048], P(('fsdp', 'rep'), 'tp')
- new_second: bfloat16 [8192, 2048], P(('fsdp', 'rep'), 'tp')
- attended: bfloat16 [4, 1024, 8192], P(None, ('fsdp', 'rep'), 'tp')
Inputs may be any that keep to these rules, and one draw needn't show every extreme that they name: `cache_lengths`: in the first row of every device's 32 rows all 256 slots are live.
All inputs are finite; a program needn't handle non-finite values.
Results may differ from a plain program's by a relative error of at most 0.0055.
Values may be sent and summed in bfloat16 or wider, within the bound.
No kernel may reach another device: no remote copies, remote signals or barrier semaphores. Data moves between devices by JAX's collectives and lax.ppermute only.
A program may use at most 128 MiB of HBM per device.

v0:
```python
import functools
import math

import jax
import jax.numpy as jnp
from jax import lax
from jax.experimental import pallas as pl
from jax.experimental.pallas import tpu as pltpu
from jax.sharding import PartitionSpec as P

HEADS = 64
KVH = 8
HD = 128
ADAM_STEP = 100

learn_rate = 0.001
beta_one = 0.9
beta_two = 0.95
decay_rate = 0.1
tiny_term = 1e-08

NY, NX, NZ = 4, 4, 8
AXES = ("fsdp", "tp", "rep")
VMEM_LIMIT = 40 * 1024 * 1024
f32 = jnp.float32
bf16 = jnp.bfloat16


def pairs_of(move):
    pairs = []
    for y in range(NY):
        for k in range(2):
            for x in range(NX):
                for z in range(NZ):
                    v, j, u, w = move(y, k, x, z)
                    source = ((y * 2 + k) * NZ + z) * NX + x
                    target = (((v % NY) * 2 + j) * NZ + w % NZ) * NX + u % NX
                    pairs.append((source, target))
    return pairs


def swap_core(a):
    return lax.ppermute(a, AXES, pairs_of(lambda y, k, x, z: (y, 1 - k, x, z)))


def pass_on(a):
    return lax.ppermute(a, AXES, pairs_of(lambda y, k, x, z: (y, k, x, z + 1 - 2 * k)))


def shift_first(a, d):
    return lax.ppermute(
        a, AXES, pairs_of(lambda y, k, x, z: (y, k, x + d, z) if k == 0 else (y + d, k, x, z))
    )


def shift_second(a, d):
    return lax.ppermute(
        a, AXES, pairs_of(lambda y, k, x, z: (y + d, k, x, z) if k == 0 else (y, k, x + d, z))
    )


def to_column(a):
    return lax.ppermute(a, AXES, pairs_of(lambda y, k, x, z: (y, k, x, z + 4 * k - y)))


def to_owner(a):
    def move(y, k, x, z):
        t = (z + y + 4 * k) % 8
        return t // 2, t % 2, x, z

    return lax.ppermute(a, AXES, pairs_of(move))


SMEM = pl.BlockSpec(memory_space=pltpu.SMEM)
VMEM = pl.BlockSpec(memory_space=pltpu.VMEM)
ANY = pl.BlockSpec(memory_space=pl.ANY)


def call(kernel, out, args, in_specs, out_specs, scratch=(), aliases=None, flops=0, moved=0):
    return pl.pallas_call(
        kernel,
        out_shape=out,
        in_specs=in_specs,
        out_specs=out_specs,
        scratch_shapes=list(scratch),
        input_output_aliases=aliases or {},
        cost_estimate=pl.CostEstimate(flops=flops, bytes_accessed=moved, transcendentals=0),
        compiler_params=pltpu.CompilerParams(vmem_limit_bytes=VMEM_LIMIT),
    )(*args)


def shape(dims, dtype):
    return jax.ShapeDtypeStruct(dims, dtype)


def after_all(value, *others):
    def kernel(*refs):
        pass

    return call(
        kernel,
        shape(value.shape, value.dtype),
        (value, *others),
        [ANY] * (1 + len(others)),
        ANY,
        aliases={0: 0},
    )


def partial_kernel(step, first, *refs):
    place, own_x, other_x, block, other_block = refs[:5]
    refs = refs[5:] if first else refs[9:]
    keep, one, two, three, token, wide, narrow, sems = refs
    k, p = place[0], place[1]
    slot = jnp.where(k == 0, step, 4 - step)
    over = (((0,), (0,)), ((), ()))
    token[...] = jnp.zeros_like(token)

    @pl.when((slot >= 0) & (slot < 4))
    def _():
        for a in range(4):
            at = slice(a * 256, a * 256 + 256)
            tile = lax.dot_general(
                block[...], own_x[:, at], over, preferred_element_type=f32
            ) + lax.dot_general(
                other_block[...], other_x[:, at], over, preferred_element_type=f32
            )
            wide[a] = tile
            narrow[a] = tile.astype(bf16)
            d = lax.rem(jnp.where(k == 0, a, slot) - p + 4, 4)
            index = jnp.where(k == 0, slot, a)

            @pl.when(d == 0)
            def _():
                pltpu.make_async_copy(wide.at[a], keep.at[index], sems.at[a]).start()

            for m, out in ((1, one), (2, two), (3, three)):

                @pl.when(d == m)
                def _():
                    pltpu.make_async_copy(narrow.at[a], out.at[index], sems.at[a]).start()

        for a in range(4):
            d = lax.rem(jnp.where(k == 0, a, slot) - p + 4, 4)
            index = jnp.where(k == 0, slot, a)

            @pl.when(d == 0)
            def _():
                pltpu.make_async_copy(wide.at[a], keep.at[index], sems.at[a]).wait()

            for m, out in ((1, one), (2, two), (3, three)):

                @pl.when(d == m)
                def _():
                    pltpu.make_async_copy(narrow.at[a], out.at[index], sems.at[a]).wait()


def middle_kernel(place, keep, one, two, three, *refs):
    own, s_one, s_two, s_three = refs[3:]
    q = place[2]
    for d, out in enumerate((own, s_one, s_two, s_three)):
        j = lax.rem(q + d, 4)
        out[...] = (
            keep[j] + one[j].astype(f32) + two[j].astype(f32) + three[j].astype(f32)
        )


def adam_kernel(gradient, master, first_moment, second_moment, *outs):
    new_master, new_first, new_second, weight = outs
    gradient = gradient[...].astype(f32).T
    first = beta_one * first_moment[...].astype(f32) + (1.0 - beta_one) * gradient
    second = beta_two * second_moment[...].astype(f32) + (1.0 - beta_two) * gradient * gradient
    corr_one = 1.0 - beta_one**ADAM_STEP
    corr_two = 1.0 - beta_two**ADAM_STEP
    update = first / corr_one / (jnp.sqrt(second / corr_two) + tiny_term)
    update = update + decay_rate * master[...]
    result = master[...] - learn_rate * update
    new_master[...] = result
    new_first[...] = first.astype(bf16)
    new_second[...] = second.astype(bf16)
    weight[...] = result.astype(bf16)


def states_kernel(place, states, kept, sent):
    k, p, q = place[0], place[1], place[2]
    for m in range(4):
        for n in range(4):
            for core, a, b, out in ((k, p, q, kept), (1 - k, q, p, sent)):
                u, v = lax.rem(a + m, 4), lax.rem(b + n, 4)
                x = jnp.where(core == 0, u, v)
                y = jnp.where(core == 0, v, u)
                at = pl.multiple_of(((2 * y + core) * 4 + x) * 256, 256)
                out[m + 4 * n] = states[:, pl.ds(at, 256)]


def project_kernel(base, n, has, kept, came, *refs):
    weights = refs[:n]
    if has:
        before_mine, before_theirs = refs[n : n + 2]
    mine, theirs = refs[-2:]
    total, other = None, None
    if has:
        total, other = before_mine[...], before_theirs[...]
    for i in range(n):
        for m in range(4):
            w = weights[i][m]
            at = base[i] * 4 + m
            term = jnp.dot(kept[at], w, preferred_element_type=f32)
            total = term if total is None else total + term
            term = jnp.dot(came[at], w, preferred_element_type=f32)
            other = term if other is None else other + term
    mine[...] = total
    theirs[...] = other


def finish_kernel(mine, theirs, queries, peak, mass, past, out):
    fresh = (mine[...] + theirs[...]).astype(bf16)
    n = fresh.shape[0]
    rows = n // 4
    group = HEADS // KVH
    line = lax.broadcasted_iota(jnp.int32, (n, n), 0)
    lane = lax.broadcasted_iota(jnp.int32, (n, n), 1)
    seen = (lax.rem(line, rows) == lax.rem(lane, rows)) & (lane <= line)
    seen = jnp.concatenate([seen.astype(f32)] * group, axis=0) > 0.5
    scale = 1.0 / math.sqrt(HD)
    keys, values = fresh[:, :HD], fresh[:, HD:]
    stack = jnp.concatenate([queries[:, g * HD : g * HD + HD] for g in range(group)], axis=0)
    scores = lax.dot_general(
        stack, keys, (((1,), (1,)), ((), ())), preferred_element_type=f32
    )
    scores = jnp.where(seen, scores * scale, -1e30)
    before = jnp.concatenate([peak[:, g : g + 1] for g in range(group)], axis=0)
    mass = jnp.concatenate([mass[:, g : g + 1] for g in range(group)], axis=0)
    top = jnp.maximum(before, jnp.max(scores, axis=1, keepdims=True))
    weight = jnp.where(seen, jnp.exp(scores - top), 0.0)
    fade = jnp.exp(before - top)
    total = mass * fade + jnp.sum(weight, axis=1, keepdims=True)
    probs = (weight / total).astype(bf16)
    result = jnp.dot(probs, values, preferred_element_type=f32)
    result = (result + past[...] * (fade / total)).astype(bf16)
    for g in range(group):
        out[:, g * HD : g * HD + HD] = result[g * n : g * n + n]


def past_part(queries, cache, lengths):
    steps, rows = queries.shape[0], queries.shape[1]
    span = cache.shape[1]
    group = HEADS // KVH
    block = queries.reshape(steps, rows, group, HD)
    scores = jnp.einsum(
        "srgd,rtd->srgt", block, cache[:, :, :HD], preferred_element_type=f32
    ) * (1.0 / math.sqrt(HD))
    live = jnp.arange(span, dtype=jnp.int32)[None, :] < lengths[:, None]
    scores = jnp.where(live[None, :, None, :], scores, -jnp.inf)
    peak = jnp.max(scores, axis=-1)
    weight = jnp.exp(scores - peak[..., None])
    mass = jnp.sum(weight, axis=-1)
    past = jnp.einsum(
        "srgt,rtd->gsrd", weight.astype(bf16), cache[:, :, HD:], preferred_element_type=f32
    )
    n = steps * rows
    return peak.reshape(n, group), mass.reshape(n, group), past.reshape(n * group, HD)


def body(
    train_inputs,
    kv_grads,
    master,
    first_moment,
    second_moment,
    hidden_states,
    queries,
    kv_cache,
    cache_lengths,
):
    f = lax.axis_index("fsdp")
    x = lax.axis_index("rep")
    y, k = f // 2, f % 2
    p = jnp.where(k == 0, x, y)
    q = jnp.where(k == 0, y, x)
    place = jnp.stack([k, p, q]).astype(jnp.int32)
    steps, rows, width = hidden_states.shape
    count = steps * rows

    block = kv_grads
    other_block = swap_core(kv_grads)
    other_x = swap_core(train_inputs)

    part = (4, 256, 256)
    buffers = ()
    outs = (shape(part, f32),) + (shape(part, bf16),) * 3 + (shape((8, 128), f32),)

    def add_slot(step, block, other_block, buffers):
        first = not buffers
        *buffers, token = call(
            functools.partial(partial_kernel, step, first),
            outs,
            (place, train_inputs, other_x, block, other_block, *buffers),
            [SMEM] + [VMEM] * 4 + [ANY] * len(buffers),
            [ANY] * 4 + [VMEM],
            [
                pltpu.VMEM(part, f32),
                pltpu.VMEM(part, bf16),
                pltpu.SemaphoreType.DMA((4,)),
            ],
            {} if first else {5: 0, 6: 1, 7: 2, 8: 3},
            flops=4 * 640 * 1024 * 256,
            moved=6 << 20,
        )
        return tuple(buffers), token

    kept, sent = call(
        states_kernel,
        (shape((16, count, 256), bf16),) * 2,
        (place, hidden_states.reshape(count, width)),
        [SMEM, VMEM],
        [VMEM, VMEM],
        moved=4 << 20,
    )
    tokens = []
    arrived = (block, other_block)
    for step in range(5):
        if step == 1:
            arrived = (after_all(arrived[0], kept), arrived[1])
        if step == 2:
            arrived = (after_all(arrived[0], tokens[0]), arrived[1])
        if step == 3:
            arrived = (after_all(arrived[0], tokens[1]), arrived[1])
        if step < 4:
            after = (pass_on(arrived[0]), pass_on(arrived[1]))
        buffers, token = add_slot(step, *arrived, buffers)
        tokens.append(token)
        arrived = after
    came = swap_core(sent)

    keep, one, two, three = buffers
    peak, mass, past = past_part(queries, kv_cache, cache_lengths)
    one, two, three = shift_first(one, 1), shift_first(two, 2), shift_first(three, 3)
    square = shape((256, 256), f32)
    own, one, two, three = call(
        middle_kernel,
        (square,) * 4,
        (place, keep, one, two, three, past, peak, mass),
        [SMEM] + [VMEM] * 4 + [ANY] * 3,
        [VMEM] * 4,
        moved=4 << 20,
    )
    one, two, three = shift_second(one, 1), shift_second(two, 2), shift_second(three, 3)
    gradient = (own + one + two + three).astype(bf16)
    gradient = to_owner(to_column(gradient))
    narrow = shape((256, 256), bf16)
    new_master, new_first, new_second, weight = call(
        adam_kernel,
        (square, narrow, narrow, narrow),
        (gradient, master, first_moment, second_moment),
        [VMEM] * 4,
        [VMEM] * 4,
        moved=1 << 20,
    )

    stack = jnp.stack(
        [weight, shift_first(weight, -1), shift_first(weight, 2), shift_first(weight, 1)]
    )
    ahead, across, behind = shift_second(stack, -1), shift_second(stack, 2), shift_second(stack, 1)
    result = (shape((count, 256), f32),) * 2

    def project(base, weights, before):
        return call(
            functools.partial(project_kernel, base, len(base), bool(before)),
            result,
            (kept, came, *weights, *before),
            [VMEM] * (2 + len(base) + len(before)),
            [VMEM] * 2,
            flops=len(base) * 4 * 4 * 128 * 256 * 256,
            moved=len(base) << 19,
        )

    sums = project((0,), (stack,), ())
    sums = project((1, 3), (ahead, behind), sums)
    mine, theirs = project((2,), (across,), sums)
    got = swap_core(theirs)
    attended = call(
        finish_kernel,
        shape((count, queries.shape[2]), bf16),
        (mine, got, queries.reshape(count, queries.shape[2]), peak, mass, past),
        [VMEM] * 6,
        VMEM,
        moved=1 << 20,
    )
    return new_master, new_first, new_second, attended.reshape(queries.shape)


def solution(mesh):
    in_specs = (
        P(("fsdp", "rep"), "tp"),
        P(("fsdp", "rep"), "tp"),
        P(("fsdp", "rep"), "tp"),
        P(("fsdp", "rep"), "tp"),
        P(("fsdp", "rep"), "tp"),
        P(None, ("fsdp", "rep"), None),
        P(None, ("fsdp", "rep"), "tp"),
        P(("fsdp", "rep"), None, "tp"),
        P(("fsdp", "rep")),
    )
    out_specs = (
        P(("fsdp", "rep"), "tp"),
        P(("fsdp", "rep"), "tp"),
        P(("fsdp", "rep"), "tp"),
        P(None, ("fsdp", "rep"), "tp"),
    )
    return jax.shard_map(body, mesh=mesh, in_specs=in_specs, out_specs=out_specs, check_vma=False)
```

profile of v0, /device:TPU:65, one launch (start us, length us, event | category | flops | bytes accessed | tf_op | source)
XLA Modules:
  0.0 131.2 jit_solution(5321273493120353352)
XLA Ops:
  1.5 3.2 %collective-permute-done.3.refs_4_ = bf16[640,256]{1,0:T(8,128)(2,1)} collective-permute-done((bf16[640,256]{1,0:T(8,128)(2,1)}, bf16[640,256]{1,0:T(8,128)(2,1)}, u32[]{:S(2)}, u32[]{:S(2)}) %collective-permute-start.3) | collective-permute-done | bytes 327712 | tf_op jit(solution)/shard_map/ppermute | solution.py:43
  4.7 1.4 %collective-permute-start.1 = (bf16[640,256]{1,0:T(8,128)(2,1)}, bf16[640,256]{1,0:T(8,128)(2,1)S(1)}, u32[]{:S(2)}, u32[]{:S(2)}) collective-permute-start(bf16[640,256]{1,0:T(8,128)(2,1)} %refs_3_.1), channel_id=1, source_target_pairs={{0,4},{4,8},{8,12},{12,16},{16,20},{20,24},{24,28},{28,0},{1,5},{5... | collective-permute-start | bytes 983048 | tf_op jit(solution)/shard_map/ppermute | solution.py:47
  6.1 5.2 %collective-permute-done.5.refs_4_ = bf16[640,256]{1,0:T(8,128)(2,1)S(1)} collective-permute-done((bf16[640,256]{1,0:T(8,128)(2,1)}, bf16[640,256]{1,0:T(8,128)(2,1)S(1)}, u32[]{:S(2)}, u32[]{:S(2)}) %collective-permute-start.5) | collective-permute-done | bytes 327712 | tf_op jit(solution)/shard_map/ppermute | solution.py:47
  11.4 1.6 %copy-done.1 = bf16[4,32,8192]{2,1,0:T(8,128)(2,1)S(1)} copy-done((bf16[4,32,8192]{2,1,0:T(8,128)(2,1)S(1)}, bf16[4,32,8192]{2,1,0:T(8,128)(2,1)}, u32[]{:S(2)}) %copy-start.1) | copy-done | bytes 2097176
  14.9 2.1 %collective-permute-start.2 = (bf16[640,256]{1,0:T(8,128)(2,1)S(1)}, bf16[640,256]{1,0:T(8,128)(2,1)S(1)}, u32[]{:S(2)}, u32[]{:S(2)}) collective-permute-start(bf16[640,256]{1,0:T(8,128)(2,1)S(1)} %shard_map.121.refs_3_), channel_id=1, source_target_pairs={{0,4},{4,8},{8,12},{12,16},{16,20},{20,24},{24,28},{28,0},{1,5},{5... | collective-permute-start | bytes 983048 | tf_op jit(solution)/shard_map/ppermute | solution.py:47
  16.9 1.7 %collective-permute-done.7.refs_4_ = bf16[640,256]{1,0:T(8,128)(2,1)S(1)} collective-permute-done((bf16[640,256]{1,0:T(8,128)(2,1)S(1)}, bf16[640,256]{1,0:T(8,128)(2,1)S(1)}, u32[]{:S(2)}, u32[]{:S(2)}) %collective-permute-start.7) | collective-permute-done | bytes 327712 | tf_op jit(solution)/shard_map/ppermute | solution.py:47
  22.2 1.8 %collective-permute-start.4 = (bf16[640,256]{1,0:T(8,128)(2,1)S(1)}, bf16[640,256]{1,0:T(8,128)(2,1)S(1)}, u32[]{:S(2)}, u32[]{:S(2)}) collective-permute-start(bf16[640,256]{1,0:T(8,128)(2,1)S(1)} %shard_map.123.refs_3_), channel_id=1, source_target_pairs={{0,4},{4,8},{8,12},{12,16},{16,20},{20,24},{24,28},{28,0},{1,5},{5... | collective-permute-start | bytes 983048 | tf_op jit(solution)/shard_map/ppermute | solution.py:47
  24.0 1.8 %collective-permute-done.8.refs_4_ = bf16[640,256]{1,0:T(8,128)(2,1)S(1)} collective-permute-done((bf16[640,256]{1,0:T(8,128)(2,1)S(1)}, bf16[640,256]{1,0:T(8,128)(2,1)S(1)}, u32[]{:S(2)}, u32[]{:S(2)}) %collective-permute-start.8) | collective-permute-done | bytes 327712 | tf_op jit(solution)/shard_map/ppermute | solution.py:47
  25.8 1.7 %collective-permute-start.9 = (bf16[640,256]{1,0:T(8,128)(2,1)S(1)}, bf16[640,256]{1,0:T(8,128)(2,1)S(1)}, u32[]{:S(2)}, u32[]{:S(2)}) collective-permute-start(bf16[640,256]{1,0:T(8,128)(2,1)S(1)} %collective-permute-done.8.refs_4_), channel_id=1, source_target_pairs={{0,4},{4,8},{8,12},{12,16},{16,20},{20,24},{24,28},{28,0},{1,5},{5... | collective-permute-start | bytes 983048 | tf_op jit(solution)/shard_map/ppermute | solution.py:47
  27.5 3.6 %shard_map.124 = (f32[4,256,256]{2,1,0:T(8,128)S(1)}, bf16[4,256,256]{2,1,0:T(8,128)(2,1)S(1)}, bf16[4,256,256]{2,1,0:T(8,128)(2,1)S(1)}, bf16[4,256,256]{2,1,0:T(8,128)(2,1)S(1)}, f32[8,128]{1,0:T(8,128)S(1)}) custom-call(s32[3]{0:T(128)S(1)} %pad_add_fusion.place.refs_0_, ...), custom_call_target="tpu_custom_call", output_to_operand_aliasing={{0}: (5, {}), {1}: (6, {}), {2}: (7, {}), {3}: (8, {})} | custom-call | flops 671088640 | bytes 6291456 | tf_op jit(solution)/shard_map/pallas_call | solution.py:80
  31.1 2.3 %collective-permute-start.6 = (bf16[640,256]{1,0:T(8,128)(2,1)S(1)}, bf16[640,256]{1,0:T(8,128)(2,1)S(1)}, u32[]{:S(2)}, u32[]{:S(2)}) collective-permute-start(bf16[640,256]{1,0:T(8,128)(2,1)S(1)} %shard_map.125.refs_3_), channel_id=1, source_target_pairs={{0,4},{4,8},{8,12},{12,16},{16,20},{20,24},{24,28},{28,0},{1,5},{5... | collective-permute-start | bytes 983048 | tf_op jit(solution)/shard_map/ppermute | solution.py:47
  33.5 4.4 %shard_map.126 = (f32[4,256,256]{2,1,0:T(8,128)S(1)}, bf16[4,256,256]{2,1,0:T(8,128)(2,1)S(1)}, bf16[4,256,256]{2,1,0:T(8,128)(2,1)S(1)}, bf16[4,256,256]{2,1,0:T(8,128)(2,1)S(1)}, f32[8,128]{1,0:T(8,128)}) custom-call(s32[3]{0:T(128)S(1)} %pad_add_fusion.place.refs_0_, ...), custom_call_target="tpu_custom_call", output_to_operand_aliasing={{0}: (5, {}), {1}: (6, {}), {2}: (7, {}), {3}: (8, {})} | custom-call | flops 671088640 | bytes 6291456 | tf_op jit(solution)/shard_map/pallas_call | solution.py:80
  37.9 4.2 %shard_map.127 = (f32[4,256,256]{2,1,0:T(8,128)S(1)}, bf16[4,256,256]{2,1,0:T(8,128)(2,1)S(1)}, bf16[4,256,256]{2,1,0:T(8,128)(2,1)S(1)}, bf16[4,256,256]{2,1,0:T(8,128)(2,1)S(1)}, f32[8,128]{1,0:T(8,128)}) custom-call(s32[3]{0:T(128)S(1)} %pad_add_fusion.place.refs_0_, ...), custom_call_target="tpu_custom_call", output_to_operand_aliasing={{0}: (5, {}), {1}: (6, {}), {2}: (7, {}), {3}: (8, {})} | custom-call | flops 671088640 | bytes 6291456 | tf_op jit(solution)/shard_map/pallas_call | solution.py:80
  42.1 3.6 %shard_map.128 = (f32[4,256,256]{2,1,0:T(8,128)S(1)}, bf16[4,256,256]{2,1,0:T(8,128)(2,1)S(1)}, bf16[4,256,256]{2,1,0:T(8,128)(2,1)S(1)}, bf16[4,256,256]{2,1,0:T(8,128)(2,1)S(1)}, f32[8,128]{1,0:T(8,128)}) custom-call(s32[3]{0:T(128)S(1)} %pad_add_fusion.place.refs_0_, ...), custom_call_target="tpu_custom_call", output_to_operand_aliasing={{0}: (5, {}), {1}: (6, {}), {2}: (7, {}), {3}: (8, {})} | custom-call | flops 671088640 | bytes 6291456 | tf_op jit(solution)/shard_map/pallas_call | solution.py:80
  45.8 1.4 %collective-permute-start.10 = (bf16[4,256,256]{2,1,0:T(8,128)(2,1)S(1)}, bf16[4,256,256]{2,1,0:T(8,128)(2,1)S(1)}, u32[]{:S(2)}, u32[]{:S(2)}) collective-permute-start(bf16[4,256,256]{2,1,0:T(8,128)(2,1)S(1)} %get-tuple-element.62), channel_id=1, source_target_pairs={{0,1},{4,5},{8,9},{12,13},{16,17},{20,21},{24,25},{28,29},{1,2},{5... | collective-permute-start | bytes 1572872 | tf_op jit(solution)/shard_map/ppermute | solution.py:51
  47.1 2.6 %collective-permute-start.11 = (bf16[4,256,256]{2,1,0:T(8,128)(2,1)S(1)}, bf16[4,256,256]{2,1,0:T(8,128)(2,1)S(1)}, u32[]{:S(2)}, u32[]{:S(2)}) collective-permute-start(bf16[4,256,256]{2,1,0:T(8,128)(2,1)S(1)} %get-tuple-element.63), channel_id=1, source_target_pairs={{0,2},{4,6},{8,10},{12,14},{16,18},{20,22},{24,26},{28,30},{1,3},{... | collective-permute-start | bytes 1572872 | tf_op jit(solution)/shard_map/ppermute | solution.py:51
  53.0 2.4 %collective-permute-done.10.one = bf16[4,256,256]{2,1,0:T(8,128)(2,1)S(1)} collective-permute-done((bf16[4,256,256]{2,1,0:T(8,128)(2,1)S(1)}, bf16[4,256,256]{2,1,0:T(8,128)(2,1)S(1)}, u32[]{:S(2)}, u32[]{:S(2)}) %collective-permute-start.10) | collective-permute-done | bytes 524320 | tf_op jit(solution)/shard_map/ppermute | solution.py:51
  55.4 6.8 %collective-permute-done.11.two = bf16[4,256,256]{2,1,0:T(8,128)(2,1)S(1)} collective-permute-done((bf16[4,256,256]{2,1,0:T(8,128)(2,1)S(1)}, bf16[4,256,256]{2,1,0:T(8,128)(2,1)S(1)}, u32[]{:S(2)}, u32[]{:S(2)}) %collective-permute-start.11) | collective-permute-done | bytes 524320 | tf_op jit(solution)/shard_map/ppermute | solution.py:51
  64.0 2.4 %collective-permute-start.14 = (f32[256,256]{1,0:T(8,128)S(1)}, f32[256,256]{1,0:T(8,128)S(1)}, u32[]{:S(2)}, u32[]{:S(2)}) collective-permute-start(f32[256,256]{1,0:T(8,128)S(1)} %get-tuple-element.67), channel_id=1, source_target_pairs={{0,128},{4,132},{8,136},{12,140},{16,144},{20,148},{24,152},{28,15... | collective-permute-start | bytes 786440 | tf_op jit(solution)/shard_map/ppermute | solution.py:57
  67.6 4.3 %collective-permute-start.18 = (bf16[16,128,256]{2,1,0:T(8,128)(2,1)S(1)}, bf16[16,128,256]{2,1,0:T(8,128)(2,1)S(1)}, u32[]{:S(2)}, u32[]{:S(2)}) collective-permute-start(bf16[16,128,256]{2,1,0:T(8,128)(2,1)S(1)} %get-tuple-element.72), channel_id=1, source_target_pairs={{0,32},{4,36},{8,40},{12,44},{16,48},{20,52},{24,56},{28,60},{1,33... | collective-permute-start | bytes 3145736 | tf_op jit(solution)/shard_map/ppermute | solution.py:43
  73.3 3.6 %collective-permute-start.16 = (bf16[256,256]{1,0:T(8,128)(2,1)S(1)}, bf16[256,256]{1,0:T(8,128)(2,1)S(1)}, u32[]{:S(2)}, u32[]{:S(2)}) collective-permute-start(bf16[256,256]{1,0:T(8,128)(2,1)S(1)} %add_convert_fusion), channel_id=1, source_target_pairs={{0,0},{4,4},{8,8},{12,12},{16,16},{20,20},{24,24},{28,28},{1,1},{5... | collective-permute-start | bytes 393224 | tf_op jit(solution)/shard_map/ppermute | solution.py:63
  76.9 6.1 %collective-permute-done.16 = bf16[256,256]{1,0:T(8,128)(2,1)S(1)} collective-permute-done((bf16[256,256]{1,0:T(8,128)(2,1)S(1)}, bf16[256,256]{1,0:T(8,128)(2,1)S(1)}, u32[]{:S(2)}, u32[]{:S(2)}) %collective-permute-start.16) | collective-permute-done | bytes 131104 | tf_op jit(solution)/shard_map/ppermute | solution.py:63
  82.9 10.9 %collective-permute-start.17 = (bf16[256,256]{1,0:T(8,128)(2,1)S(1)}, bf16[256,256]{1,0:T(8,128)(2,1)S(1)}, u32[]{:S(2)}, u32[]{:S(2)}) collective-permute-start(bf16[256,256]{1,0:T(8,128)(2,1)S(1)} %collective-permute-done.16), channel_id=1, source_target_pairs={{0,0},{4,36},{8,72},{12,108},{16,144},{20,180},{24,216},{28,252},{... | collective-permute-start | bytes 393224 | tf_op jit(solution)/shard_map/ppermute | solution.py:71
  93.9 1.9 %collective-permute-done.17.gradient = bf16[256,256]{1,0:T(8,128)(2,1)S(1)} collective-permute-done((bf16[256,256]{1,0:T(8,128)(2,1)S(1)}, bf16[256,256]{1,0:T(8,128)(2,1)S(1)}, u32[]{:S(2)}, u32[]{:S(2)}) %collective-permute-start.17) | collective-permute-done | bytes 131104 | tf_op jit(solution)/shard_map/ppermute | solution.py:71
  96.9 1.9 %collective-permute-start.20 = (bf16[256,256]{1,0:T(8,128)(2,1)S(1)}, bf16[256,256]{1,0:T(8,128)(2,1)S(1)}, u32[]{:S(2)}, u32[]{:S(2)}) collective-permute-start(bf16[256,256]{1,0:T(8,128)(2,1)S(1)} %get-tuple-element.73), channel_id=1, source_target_pairs={{0,2},{4,6},{8,10},{12,14},{16,18},{20,22},{24,26},{28,30},{1,3},{... | collective-permute-start | bytes 393224 | tf_op jit(solution)/shard_map/ppermute | solution.py:51
  102.2 1.6 %collective-permute-done.21 = bf16[256,256]{1,0:T(8,128)(2,1)S(1)} collective-permute-done((bf16[256,256]{1,0:T(8,128)(2,1)S(1)}, bf16[256,256]{1,0:T(8,128)(2,1)S(1)}, u32[]{:S(2)}, u32[]{:S(2)}) %collective-permute-start.21) | collective-permute-done | bytes 131104 | tf_op jit(solution)/shard_map/ppermute | solution.py:51
  103.9 2.6 %collective-permute-start.23 = (bf16[4,256,256]{2,1,0:T(8,128)(2,1)S(1)}, bf16[4,256,256]{2,1,0:T(8,128)(2,1)S(1)}, u32[]{:S(2)}, u32[]{:S(2)}) collective-permute-start(bf16[4,256,256]{2,1,0:T(8,128)(2,1)S(1)} %pad_maximum_fusion.refs_0_), channel_id=1, source_target_pairs={{0,192},{4,196},{8,200},{12,204},{16,208},{20,212},{24,216},{28,22... | collective-permute-start | bytes 1572872 | tf_op jit(solution)/shard_map/ppermute | solution.py:57
  106.5 1.6 %collective-permute-start.22 = (bf16[4,256,256]{2,1,0:T(8,128)(2,1)S(1)}, bf16[4,256,256]{2,1,0:T(8,128)(2,1)S(1)}, u32[]{:S(2)}, u32[]{:S(2)}) collective-permute-start(bf16[4,256,256]{2,1,0:T(8,128)(2,1)S(1)} %pad_maximum_fusion.refs_0_), channel_id=1, source_target_pairs={{0,128},{4,132},{8,136},{12,140},{16,144},{20,148},{24,152},{28,15... | collective-permute-start | bytes 1572872 | tf_op jit(solution)/shard_map/ppermute | solution.py:57
  108.4 9.9 %collective-permute-done.23.refs_0_ = bf16[4,256,256]{2,1,0:T(8,128)(2,1)S(1)} collective-permute-done((bf16[4,256,256]{2,1,0:T(8,128)(2,1)S(1)}, bf16[4,256,256]{2,1,0:T(8,128)(2,1)S(1)}, u32[]{:S(2)}, u32[]{:S(2)}) %collective-permute-start.23) | collective-permute-done | bytes 524320 | tf_op jit(solution)/shard_map/ppermute | solution.py:57
  118.3 3.4 %collective-permute-done.24.refs_1_ = bf16[4,256,256]{2,1,0:T(8,128)(2,1)S(1)} collective-permute-done((bf16[4,256,256]{2,1,0:T(8,128)(2,1)S(1)}, bf16[4,256,256]{2,1,0:T(8,128)(2,1)S(1)}, u32[]{:S(2)}, u32[]{:S(2)}) %collective-permute-start.24) | collective-permute-done | bytes 524320 | tf_op jit(solution)/shard_map/ppermute | solution.py:57
  122.5 5.9 %collective-permute-start.25 = (f32[128,256]{1,0:T(8,128)S(1)}, f32[128,256]{1,0:T(8,128)S(1)}, u32[]{:S(2)}, u32[]{:S(2)}) collective-permute-start(f32[128,256]{1,0:T(8,128)S(1)} %get-tuple-element.79), channel_id=1, source_target_pairs={{0,32},{4,36},{8,40},{12,44},{16,48},{20,52},{24,56},{28,60},{1,33... | collective-permute-start | bytes 393224 | tf_op jit(solution)/shard_map/ppermute | solution.py:43
  129.4 1.9 %shard_map.134 = bf16[128,1024]{1,0:T(8,128)(2,1)} custom-call(f32[128,256]{1,0:T(8,128)S(1)} %get-tuple-element.78.mine, f32[128,256]{1,0:T(8,128)S(1)} %collective-permute-done.25.theirs, bf16[128,1024]{1,0:T(8,128)(2,1)S(1)} %bitcast.51, f32[128,8]{1,0:T(8,128)S(1)} %bitcast.53, f32[128,8]{1,0:T(8,128)S(1)} %bitcast.55, f32[1024,128]{1,0:T(8,128)S(1)} %bitcast.48), custom_call_target="tpu_custom_call" | custom-call | bytes 1048576 | tf_op jit(solution)/shard_map/pallas_call | solution.py:80
  (64 shorter events, 20.5 us)
Async XLA Ops:
  0.6 19.3 %copy-start = (bf16[640,1024]{1,0:T(8,128)(2,1)S(1)}, bf16[640,1024]{1,0:T(8,128)(2,1)}, u32[]{:S(2)}) copy-start(bf16[640,1024]{1,0:T(8,128)(2,1)} %refs_1_.9) | copy-start | bytes 3932164
  0.6 19.3 %collective-permute-start = (bf16[640,1024]{1,0:T(8,128)(2,1)}, bf16[640,1024]{1,0:T(8,128)(2,1)S(1)}, u32[]{:S(2)}, u32[]{:S(2)}) collective-permute-start(bf16[640,1024]{1,0:T(8,128)(2,1)} %refs_1_.9), channel_id=1, source_target_pairs={{0,32},{4,36},{8,40},{12,44},{16,48},{20,52},{24,56},{28,60},{1,33... | collective-permute-start | bytes 3932168 | tf_op jit(solution)/shard_map/ppermute | solution.py:43
  1.4 3.3 %collective-permute-start.3 = (bf16[640,256]{1,0:T(8,128)(2,1)}, bf16[640,256]{1,0:T(8,128)(2,1)}, u32[]{:S(2)}, u32[]{:S(2)}) collective-permute-start(bf16[640,256]{1,0:T(8,128)(2,1)} %refs_3_.1), channel_id=1, source_target_pairs={{0,32},{4,36},{8,40},{12,44},{16,48},{20,52},{24,56},{28,60},{1,33... | collective-permute-start | bytes 983048 | tf_op jit(solution)/shard_map/ppermute | solution.py:43
  4.7 6.6 %collective-permute-start.5 = (bf16[640,256]{1,0:T(8,128)(2,1)}, bf16[640,256]{1,0:T(8,128)(2,1)S(1)}, u32[]{:S(2)}, u32[]{:S(2)}) collective-permute-start(bf16[640,256]{1,0:T(8,128)(2,1)} %collective-permute-done.3.refs_4_), channel_id=1, source_target_pairs={{0,4},{4,8},{8,12},{12,16},{16,20},{20,24},{24,28},{28,0},{1,5},{5... | collective-permute-start | bytes 983048 | tf_op jit(solution)/shard_map/ppermute | solution.py:47
  4.7 10.1 %collective-permute-start.1 = (bf16[640,256]{1,0:T(8,128)(2,1)}, bf16[640,256]{1,0:T(8,128)(2,1)S(1)}, u32[]{:S(2)}, u32[]{:S(2)}) collective-permute-start(bf16[640,256]{1,0:T(8,128)(2,1)} %refs_3_.1), channel_id=1, source_target_pairs={{0,4},{4,8},{8,12},{12,16},{16,20},{20,24},{24,28},{28,0},{1,5},{5... | collective-permute-start | bytes 983048 | tf_op jit(solution)/shard_map/ppermute | solution.py:47
  11.3 7.3 %collective-permute-start.7 = (bf16[640,256]{1,0:T(8,128)(2,1)S(1)}, bf16[640,256]{1,0:T(8,128)(2,1)S(1)}, u32[]{:S(2)}, u32[]{:S(2)}) collective-permute-start(bf16[640,256]{1,0:T(8,128)(2,1)S(1)} %collective-permute-done.5.refs_4_), channel_id=1, source_target_pairs={{0,4},{4,8},{8,12},{12,16},{16,20},{20,24},{24,28},{28,0},{1,5},{5... | collective-permute-start | bytes 983048 | tf_op jit(solution)/shard_map/ppermute | solution.py:47
  14.9 9.1 %copy-start.2 = (bf16[4,32,1024]{2,1,0:T(8,128)(2,1)S(1)}, bf16[4,32,1024]{2,1,0:T(8,128)(2,1)}, u32[]{:S(2)}) copy-start(bf16[4,32,1024]{2,1,0:T(8,128)(2,1)} %param.15) | copy-start | bytes 786436
  14.9 7.3 %collective-permute-start.2 = (bf16[640,256]{1,0:T(8,128)(2,1)S(1)}, bf16[640,256]{1,0:T(8,128)(2,1)S(1)}, u32[]{:S(2)}, u32[]{:S(2)}) collective-permute-start(bf16[640,256]{1,0:T(8,128)(2,1)S(1)} %shard_map.121.refs_3_), channel_id=1, source_target_pairs={{0,4},{4,8},{8,12},{12,16},{16,20},{20,24},{24,28},{28,0},{1,5},{5... | collective-permute-start | bytes 983048 | tf_op jit(solution)/shard_map/ppermute | solution.py:47
  18.7 7.1 %collective-permute-start.8 = (bf16[640,256]{1,0:T(8,128)(2,1)S(1)}, bf16[640,256]{1,0:T(8,128)(2,1)S(1)}, u32[]{:S(2)}, u32[]{:S(2)}) collective-permute-start(bf16[640,256]{1,0:T(8,128)(2,1)S(1)} %collective-permute-done.7.refs_4_), channel_id=1, source_target_pairs={{0,4},{4,8},{8,12},{12,16},{16,20},{20,24},{24,28},{28,0},{1,5},{5... | collective-permute-start | bytes 983048 | tf_op jit(solution)/shard_map/ppermute | solution.py:47
  22.2 8.9 %collective-permute-start.4 = (bf16[640,256]{1,0:T(8,128)(2,1)S(1)}, bf16[640,256]{1,0:T(8,128)(2,1)S(1)}, u32[]{:S(2)}, u32[]{:S(2)}) collective-permute-start(bf16[640,256]{1,0:T(8,128)(2,1)S(1)} %shard_map.123.refs_3_), channel_id=1, source_target_pairs={{0,4},{4,8},{8,12},{12,16},{16,20},{20,24},{24,28},{28,0},{1,5},{5... | collective-permute-start | bytes 983048 | tf_op jit(solution)/shard_map/ppermute | solution.py:47
  25.8 16.3 %collective-permute-start.9 = (bf16[640,256]{1,0:T(8,128)(2,1)S(1)}, bf16[640,256]{1,0:T(8,128)(2,1)S(1)}, u32[]{:S(2)}, u32[]{:S(2)}) collective-permute-start(bf16[640,256]{1,0:T(8,128)(2,1)S(1)} %collective-permute-done.8.refs_4_), channel_id=1, source_target_pairs={{0,4},{4,8},{8,12},{12,16},{16,20},{20,24},{24,28},{28,0},{1,5},{5... | collective-permute-start | bytes 983048 | tf_op jit(solution)/shard_map/ppermute | solution.py:47
  31.1 11.0 %collective-permute-start.6 = (bf16[640,256]{1,0:T(8,128)(2,1)S(1)}, bf16[640,256]{1,0:T(8,128)(2,1)S(1)}, u32[]{:S(2)}, u32[]{:S(2)}) collective-permute-start(bf16[640,256]{1,0:T(8,128)(2,1)S(1)} %shard_map.125.refs_3_), channel_id=1, source_target_pairs={{0,4},{4,8},{8,12},{12,16},{16,20},{20,24},{24,28},{28,0},{1,5},{5... | collective-permute-start | bytes 983048 | tf_op jit(solution)/shard_map/ppermute | solution.py:47
  42.1 8.7 %copy-start.7 = (bf16[32,256,256]{2,1,0:T(8,128)(2,1)S(1)}, bf16[32,256,256]{2,1,0:T(8,128)(2,1)}, u32[]{:S(2)}) copy-start(bf16[32,256,256]{2,1,0:T(8,128)(2,1)} %param.16) | copy-start | bytes 12582916
  45.8 9.7 %collective-permute-start.10 = (bf16[4,256,256]{2,1,0:T(8,128)(2,1)S(1)}, bf16[4,256,256]{2,1,0:T(8,128)(2,1)S(1)}, u32[]{:S(2)}, u32[]{:S(2)}) collective-permute-start(bf16[4,256,256]{2,1,0:T(8,128)(2,1)S(1)} %get-tuple-element.62), channel_id=1, source_target_pairs={{0,1},{4,5},{8,9},{12,13},{16,17},{20,21},{24,25},{28,29},{1,2},{5... | collective-permute-start | bytes 1572872 | tf_op jit(solution)/shard_map/ppermute | solution.py:51
  47.1 15.1 %collective-permute-start.11 = (bf16[4,256,256]{2,1,0:T(8,128)(2,1)S(1)}, bf16[4,256,256]{2,1,0:T(8,128)(2,1)S(1)}, u32[]{:S(2)}, u32[]{:S(2)}) collective-permute-start(bf16[4,256,256]{2,1,0:T(8,128)(2,1)S(1)} %get-tuple-element.63), channel_id=1, source_target_pairs={{0,2},{4,6},{8,10},{12,14},{16,18},{20,22},{24,26},{28,30},{1,3},{... | collective-permute-start | bytes 1572872 | tf_op jit(solution)/shard_map/ppermute | solution.py:51
  49.8 12.5 %collective-permute-start.12 = (bf16[4,256,256]{2,1,0:T(8,128)(2,1)S(1)}, bf16[4,256,256]{2,1,0:T(8,128)(2,1)S(1)}, u32[]{:S(2)}, u32[]{:S(2)}) collective-permute-start(bf16[4,256,256]{2,1,0:T(8,128)(2,1)S(1)} %get-tuple-element.64), channel_id=1, source_target_pairs={{0,3},{4,7},{8,11},{12,15},{16,19},{20,23},{24,27},{28,31},{1,0},{... | collective-permute-start | bytes 1572872 | tf_op jit(solution)/shard_map/ppermute | solution.py:51
  62.2 33.6 %copy-start.4 = (f32[256,256]{1,0:T(8,128)S(1)}, f32[256,256]{1,0:T(8,128)}, u32[]{:S(2)}) copy-start(f32[256,256]{1,0:T(8,128)} %master.1) | copy-start | bytes 786436
  62.2 33.6 %copy-start.5 = (bf16[256,256]{1,0:T(8,128)(2,1)S(1)}, bf16[256,256]{1,0:T(8,128)(2,1)}, u32[]{:S(2)}) copy-start(bf16[256,256]{1,0:T(8,128)(2,1)} %first_moment.1) | copy-start | bytes 393220
  62.2 33.6 %copy-start.6 = (bf16[256,256]{1,0:T(8,128)(2,1)S(1)}, bf16[256,256]{1,0:T(8,128)(2,1)}, u32[]{:S(2)}) copy-start(bf16[256,256]{1,0:T(8,128)(2,1)} %second_moment.1) | copy-start | bytes 393220
  63.0 8.9 %collective-permute-start.13 = (f32[256,256]{1,0:T(8,128)S(1)}, f32[256,256]{1,0:T(8,128)S(1)}, u32[]{:S(2)}, u32[]{:S(2)}) collective-permute-start(f32[256,256]{1,0:T(8,128)S(1)} %get-tuple-element.66), channel_id=1, source_target_pairs={{0,64},{4,68},{8,72},{12,76},{16,80},{20,84},{24,88},{28,92},{1,65... | collective-permute-start | bytes 786440 | tf_op jit(solution)/shard_map/ppermute | solution.py:57
  64.0 9.0 %collective-permute-start.14 = (f32[256,256]{1,0:T(8,128)S(1)}, f32[256,256]{1,0:T(8,128)S(1)}, u32[]{:S(2)}, u32[]{:S(2)}) collective-permute-start(f32[256,256]{1,0:T(8,128)S(1)} %get-tuple-element.67), channel_id=1, source_target_pairs={{0,128},{4,132},{8,136},{12,140},{16,144},{20,148},{24,152},{28,15... | collective-permute-start | bytes 786440 | tf_op jit(solution)/shard_map/ppermute | solution.py:57
  66.5 6.7 %collective-permute-start.15 = (f32[256,256]{1,0:T(8,128)S(1)}, f32[256,256]{1,0:T(8,128)S(1)}, u32[]{:S(2)}, u32[]{:S(2)}) collective-permute-start(f32[256,256]{1,0:T(8,128)S(1)} %get-tuple-element.68), channel_id=1, source_target_pairs={{0,192},{4,196},{8,200},{12,204},{16,208},{20,212},{24,216},{28,22... | collective-permute-start | bytes 786440 | tf_op jit(solution)/shard_map/ppermute | solution.py:57
  67.6 40.5 %collective-permute-start.18 = (bf16[16,128,256]{2,1,0:T(8,128)(2,1)S(1)}, bf16[16,128,256]{2,1,0:T(8,128)(2,1)S(1)}, u32[]{:S(2)}, u32[]{:S(2)}) collective-permute-start(bf16[16,128,256]{2,1,0:T(8,128)(2,1)S(1)} %get-tuple-element.72), channel_id=1, source_target_pairs={{0,32},{4,36},{8,40},{12,44},{16,48},{20,52},{24,56},{28,60},{1,33... | collective-permute-start | bytes 3145736 | tf_op jit(solution)/shard_map/ppermute | solution.py:43
  73.3 9.6 %collective-permute-start.16 = (bf16[256,256]{1,0:T(8,128)(2,1)S(1)}, bf16[256,256]{1,0:T(8,128)(2,1)S(1)}, u32[]{:S(2)}, u32[]{:S(2)}) collective-permute-start(bf16[256,256]{1,0:T(8,128)(2,1)S(1)} %add_convert_fusion), channel_id=1, source_target_pairs={{0,0},{4,4},{8,8},{12,12},{16,16},{20,20},{24,24},{28,28},{1,1},{5... | collective-permute-start | bytes 393224 | tf_op jit(solution)/shard_map/ppermute | solution.py:63
  82.9 12.9 %collective-permute-start.17 = (bf16[256,256]{1,0:T(8,128)(2,1)S(1)}, bf16[256,256]{1,0:T(8,128)(2,1)S(1)}, u32[]{:S(2)}, u32[]{:S(2)}) collective-permute-start(bf16[256,256]{1,0:T(8,128)(2,1)S(1)} %collective-permute-done.16), channel_id=1, source_target_pairs={{0,0},{4,36},{8,72},{12,108},{16,144},{20,180},{24,216},{28,252},{... | collective-permute-start | bytes 393224 | tf_op jit(solution)/shard_map/ppermute | solution.py:71
  96.9 4.1 %collective-permute-start.19 = (bf16[256,256]{1,0:T(8,128)(2,1)S(1)}, bf16[256,256]{1,0:T(8,128)(2,1)S(1)}, u32[]{:S(2)}, u32[]{:S(2)}) collective-permute-start(bf16[256,256]{1,0:T(8,128)(2,1)S(1)} %get-tuple-element.73), channel_id=1, source_target_pairs={{0,3},{4,7},{8,11},{12,15},{16,19},{20,23},{24,27},{28,31},{1,0},{... | collective-permute-start | bytes 393224 | tf_op jit(solution)/shard_map/ppermute | solution.py:51
  96.9 5.3 %collective-permute-start.20 = (bf16[256,256]{1,0:T(8,128)(2,1)S(1)}, bf16[256,256]{1,0:T(8,128)(2,1)S(1)}, u32[]{:S(2)}, u32[]{:S(2)}) collective-permute-start(bf16[256,256]{1,0:T(8,128)(2,1)S(1)} %get-tuple-element.73), channel_id=1, source_target_pairs={{0,2},{4,6},{8,10},{12,14},{16,18},{20,22},{24,26},{28,30},{1,3},{... | collective-permute-start | bytes 393224 | tf_op jit(solution)/shard_map/ppermute | solution.py:51
  98.8 5.0 %collective-permute-start.21 = (bf16[256,256]{1,0:T(8,128)(2,1)S(1)}, bf16[256,256]{1,0:T(8,128)(2,1)S(1)}, u32[]{:S(2)}, u32[]{:S(2)}) collective-permute-start(bf16[256,256]{1,0:T(8,128)(2,1)S(1)} %get-tuple-element.73), channel_id=1, source_target_pairs={{0,1},{4,5},{8,9},{12,13},{16,17},{20,21},{24,25},{28,29},{1,2},{5... | collective-permute-start | bytes 393224 | tf_op jit(solution)/shard_map/ppermute | solution.py:51
  103.9 14.4 %collective-permute-start.23 = (bf16[4,256,256]{2,1,0:T(8,128)(2,1)S(1)}, bf16[4,256,256]{2,1,0:T(8,128)(2,1)S(1)}, u32[]{:S(2)}, u32[]{:S(2)}) collective-permute-start(bf16[4,256,256]{2,1,0:T(8,128)(2,1)S(1)} %pad_maximum_fusion.refs_0_), channel_id=1, source_target_pairs={{0,192},{4,196},{8,200},{12,204},{16,208},{20,212},{24,216},{28,22... | collective-permute-start | bytes 1572872 | tf_op jit(solution)/shard_map/ppermute | solution.py:57
  106.5 15.2 %collective-permute-start.24 = (bf16[4,256,256]{2,1,0:T(8,128)(2,1)S(1)}, bf16[4,256,256]{2,1,0:T(8,128)(2,1)S(1)}, u32[]{:S(2)}, u32[]{:S(2)}) collective-permute-start(bf16[4,256,256]{2,1,0:T(8,128)(2,1)S(1)} %pad_maximum_fusion.refs_0_), channel_id=1, source_target_pairs={{0,64},{4,68},{8,72},{12,76},{16,80},{20,84},{24,88},{28,92},{1,65... | collective-permute-start | bytes 1572872 | tf_op jit(solution)/shard_map/ppermute | solution.py:57
  106.5 15.6 %collective-permute-start.22 = (bf16[4,256,256]{2,1,0:T(8,128)(2,1)S(1)}, bf16[4,256,256]{2,1,0:T(8,128)(2,1)S(1)}, u32[]{:S(2)}, u32[]{:S(2)}) collective-permute-start(bf16[4,256,256]{2,1,0:T(8,128)(2,1)S(1)} %pad_maximum_fusion.refs_0_), channel_id=1, source_target_pairs={{0,128},{4,132},{8,136},{12,140},{16,144},{20,148},{24,152},{28,15... | collective-permute-start | bytes 1572872 | tf_op jit(solution)/shard_map/ppermute | solution.py:57
  122.5 6.9 %collective-permute-start.25 = (f32[128,256]{1,0:T(8,128)S(1)}, f32[128,256]{1,0:T(8,128)S(1)}, u32[]{:S(2)}, u32[]{:S(2)}) collective-permute-start(f32[128,256]{1,0:T(8,128)S(1)} %get-tuple-element.79), channel_id=1, source_target_pairs={{0,32},{4,36},{8,40},{12,44},{16,48},{20,52},{24,56},{28,60},{1,33... | collective-permute-start | bytes 393224 | tf_op jit(solution)/shard_map/ppermute | solution.py:43
  (3 other events, 14.4 us)
where the time goes:
time: 131 us
  starting transfers between devices  52.7 us (40%)
  waiting for transfers between devices  51.1 us (39%)
  Pallas kernels  22.5 us (17%)
  local copies, waits for them, and re-layouts  1.99 us (2%)
  matrix products  1.35 us (1%)
    pallas_call x15, Pallas kernels, call(): pl.pallas_call(kernel, out_shape=out, in_specs=in_specs, out_specs=out_sp...  22.5 us
    ppermute x6, waiting for transfers between devices, shift_second(): lax.ppermute(a, AXES, pairs_of(lambda y, k, x, z: (y + d, k, x, z) if k =...  14.5 us
    ppermute x6, waiting for transfers between devices, shift_first(): lax.ppermute(a, AXES, pairs_of(lambda y, k, x, z: (y, k, x + d, z) if k =...  13.4 us
    ppermute x4, starting transfers between devices, swap_core(): return lax.ppermute(a, AXES, pairs_of(lambda y, k, x, z: (y, 1 - k, x, z)))  11.1 us
    ppermute x1, starting transfers between devices, to_owner(): return lax.ppermute(a, AXES, pairs_of(move))  10.9 us
    ppermute x8, waiting for transfers between devices, pass_on(): lax.ppermute(a, AXES, pairs_of(lambda y, k, x, z: (y, k, x, z + 1 - 2 * k)))  10.9 us
    ppermute x8, starting transfers between devices, pass_on(): lax.ppermute(a, AXES, pairs_of(lambda y, k, x, z: (y, k, x, z + 1 - 2 * k)))  10.5 us
    ppermute x6, starting transfers between devices, shift_second(): lax.ppermute(a, AXES, pairs_of(lambda y, k, x, z: (y + d, k, x, z) if k =...  8.8 us
  transfers between devices with their start and end apart: 26, of which 18 were waited for; matrix products, arithmetic and copies ran while one was open for 2% of the time, Pallas kernels for 12%

commit v1 on v0

--- a/solution.py
+++ b/solution.py
@@ -59,16 +59,10 @@
     )
 
 
-def to_column(a):
-    return lax.ppermute(a, AXES, pairs_of(lambda y, k, x, z: (y, k, x, z + 4 * k - y)))
-
-
 def to_owner(a):
-    def move(y, k, x, z):
-        t = (z + y + 4 * k) % 8
-        return t // 2, t % 2, x, z
-
-    return lax.ppermute(a, AXES, pairs_of(move))
+    return lax.ppermute(
+        a, AXES, pairs_of(lambda y, k, x, z: (z // 2, z % 2, x, z + 4 * k - y))
+    )
 
 
 SMEM = pl.BlockSpec(memory_space=pltpu.SMEM)
@@ -109,50 +103,30 @@
 
 def partial_kernel(step, first, *refs):
     place, own_x, other_x, block, other_block = refs[:5]
-    refs = refs[5:] if first else refs[9:]
-    keep, one, two, three, token, wide, narrow, sems = refs
+    keep, one, two, three, token = refs[5:] if first else refs[9:]
     k, p = place[0], place[1]
     slot = jnp.where(k == 0, step, 4 - step)
-    over = (((0,), (0,)), ((), ()))
     token[...] = jnp.zeros_like(token)
 
     @pl.when((slot >= 0) & (slot < 4))
     def _():
+        mine, theirs = block[...].T, other_block[...].T
         for a in range(4):
             at = slice(a * 256, a * 256 + 256)
-            tile = lax.dot_general(
-                block[...], own_x[:, at], over, preferred_element_type=f32
-            ) + lax.dot_general(
-                other_block[...], other_x[:, at], over, preferred_element_type=f32
-            )
-            wide[a] = tile
-            narrow[a] = tile.astype(bf16)
+            tile = jnp.dot(mine, own_x[:, at], preferred_element_type=f32)
+            tile = tile + jnp.dot(theirs, other_x[:, at], preferred_element_type=f32)
             d = lax.rem(jnp.where(k == 0, a, slot) - p + 4, 4)
             index = jnp.where(k == 0, slot, a)
 
             @pl.when(d == 0)
             def _():
-                pltpu.make_async_copy(wide.at[a], keep.at[index], sems.at[a]).start()
+                keep[index] = tile
 
             for m, out in ((1, one), (2, two), (3, three)):
 
                 @pl.when(d == m)
                 def _():
-                    pltpu.make_async_copy(narrow.at[a], out.at[index], sems.at[a]).start()
-
-        for a in range(4):
-            d = lax.rem(jnp.where(k == 0, a, slot) - p + 4, 4)
-            index = jnp.where(k == 0, slot, a)
-
-            @pl.when(d == 0)
-            def _():
-                pltpu.make_async_copy(wide.at[a], keep.at[index], sems.at[a]).wait()
-
-            for m, out in ((1, one), (2, two), (3, three)):
-
-                @pl.when(d == m)
-                def _():
-                    pltpu.make_async_copy(narrow.at[a], out.at[index], sems.at[a]).wait()
+                    out[index] = tile.astype(bf16)
 
 
 def middle_kernel(place, keep, one, two, three, *refs):
@@ -296,13 +270,9 @@
             functools.partial(partial_kernel, step, first),
             outs,
             (place, train_inputs, other_x, block, other_block, *buffers),
-            [SMEM] + [VMEM] * 4 + [ANY] * len(buffers),
-            [ANY] * 4 + [VMEM],
-            [
-                pltpu.VMEM(part, f32),
-                pltpu.VMEM(part, bf16),
-                pltpu.SemaphoreType.DMA((4,)),
-            ],
+            [SMEM] + [VMEM] * (4 + len(buffers)),
+            [VMEM] * 5,
+            (),
             {} if first else {5: 0, 6: 1, 7: 2, 8: 3},
             flops=4 * 640 * 1024 * 256,
             moved=6 << 20,
@@ -321,11 +291,11 @@
     arrived = (block, other_block)
     for step in range(5):
         if step == 1:
-            arrived = (after_all(arrived[0], kept), arrived[1])
+            arrived = (arrived[0], after_all(arrived[1], kept))
         if step == 2:
-            arrived = (after_all(arrived[0], tokens[0]), arrived[1])
+            arrived = (arrived[0], after_all(arrived[1], tokens[0]))
         if step == 3:
-            arrived = (after_all(arrived[0], tokens[1]), arrived[1])
+            arrived = (arrived[0], after_all(arrived[1], tokens[1]))
         if step < 4:
             after = (pass_on(arrived[0]), pass_on(arrived[1]))
         buffers, token = add_slot(step, *arrived, buffers)
@@ -347,7 +317,7 @@
     )
     one, two, three = shift_second(one, 1), shift_second(two, 2), shift_second(three, 3)
     gradient = (own + one + two + three).astype(bf16)
-    gradient = to_owner(to_column(gradient))
+    gradient = to_owner(gradient)
     narrow = shape((256, 256), bf16)
     new_master, new_first, new_second, weight = call(
         adam_kernel,

time: 131 us -> 121 us (0.924)
  waiting for transfers between devices: 51.1 us -> 44.8 us
  Pallas kernels: 22.5 us -> 19.9 us
    ppermute x4, starting transfers between devices: 11.1 us -> 17.6 us  [swap_core(): return lax.ppermute(a, AXES, pairs_of(lambda y, k, x, z: (y, 1 - k, x, z)))]
    ppermute x2 -> x1, starting transfers between devices: 14.5 us -> 9.38 us  [to_owner(): lax.ppermute(a, AXES, pairs_of(lambda y, k, x, z: (z // 2, z % 2, x, z +...]
    ppermute x2 -> x1, waiting for transfers between devices: 7.99 us -> 3.29 us  [to_owner(): lax.ppermute(a, AXES, pairs_of(lambda y, k, x, z: (z // 2, z % 2, x, z +...]
    pallas_call x15, Pallas kernels: 22.5 us -> 19.9 us  [call(): pl.pallas_call(kernel, out_shape=out, in_specs=in_specs, out_specs=out_sp...]
    ppermute x8, waiting for transfers between devices: 10.9 us -> 9.11 us  [pass_on(): lax.ppermute(a, AXES, pairs_of(lambda y, k, x, z: (y, k, x, z + 1 - 2 * k)))]
    ppermute x8, starting transfers between devices: 10.5 us -> 9.08 us  [pass_on(): lax.ppermute(a, AXES, pairs_of(lambda y, k, x, z: (y, k, x, z + 1 - 2 * k)))]
  transfers between devices with their start and end apart: 26 -> 25, of which waited for: 18 -> 17; matrix products, arithmetic and copies ran while one was open for 2% -> 2% of each run, Pallas kernels for 12% -> 11%
where the time goes in v1:
time: 121 us
  starting transfers between devices  51.6 us (43%)
  waiting for transfers between devices  44.8 us (37%)
  Pallas kernels  19.9 us (16%)
  local copies, waits for them, and re-layouts  1.99 us (2%)
  matrix products  1.36 us (1%)
    pallas_call x15, Pallas kernels, call(): pl.pallas_call(kernel, out_shape=out, in_specs=in_specs, out_specs=out_sp...  19.9 us
    ppermute x4, starting transfers between devices, swap_core(): return lax.ppermute(a, AXES, pairs_of(lambda y, k, x, z: (y, 1 - k, x, z)))  17.6 us
    ppermute x6, waiting for transfers between devices, shift_first(): lax.ppermute(a, AXES, pairs_of(lambda y, k, x, z: (y, k, x + d, z) if k =...  14.4 us
    ppermute x6, waiting for transfers between devices, shift_second(): lax.ppermute(a, AXES, pairs_of(lambda y, k, x, z: (y + d, k, x, z) if k =...  13.7 us
    ppermute x1, starting transfers between devices, to_owner(): lax.ppermute(a, AXES, pairs_of(lambda y, k, x, z: (z // 2, z % 2, x, z +...  9.38 us
    ppermute x8, waiting for transfers between devices, pass_on(): lax.ppermute(a, AXES, pairs_of(lambda y, k, x, z: (y, k, x, z + 1 - 2 * k)))  9.11 us
    ppermute x8, starting transfers between devices, pass_on(): lax.ppermute(a, AXES, pairs_of(lambda y, k, x, z: (y, k, x, z + 1 - 2 * k)))  9.08 us
    ppermute x6, starting transfers between devices, shift_second(): lax.ppermute(a, AXES, pairs_of(lambda y, k, x, z: (y + d, k, x, z) if k =...  8.44 us
  transfers between devices with their start and end apart: 25, of which 17 were waited for; matrix products, arithmetic and copies ran while one was open for 2% of the time, Pallas kernels for 11%

profile of v1, /device:TPU:65, one launch (start us, length us, event | category | flops | bytes accessed | tf_op | source)
XLA Modules:
  0.0 121.2 jit_solution(15067532108961542992)
XLA Ops:
  1.5 3.2 %collective-permute-done.5.refs_4_ = bf16[640,256]{1,0:T(8,128)(2,1)} collective-permute-done((bf16[640,256]{1,0:T(8,128)(2,1)}, bf16[640,256]{1,0:T(8,128)(2,1)}, u32[]{:S(2)}, u32[]{:S(2)}) %collective-permute-start.5) | collective-permute-done | bytes 327712 | tf_op jit(solution)/shard_map/ppermute | solution.py:43
  4.7 3.4 %collective-permute-done.1.refs_3_ = bf16[640,256]{1,0:T(8,128)(2,1)S(1)} collective-permute-done((bf16[640,256]{1,0:T(8,128)(2,1)}, bf16[640,256]{1,0:T(8,128)(2,1)S(1)}, u32[]{:S(2)}, u32[]{:S(2)}) %collective-permute-start.1) | collective-permute-done | bytes 327712 | tf_op jit(solution)/shard_map/ppermute | solution.py:47
  8.2 1.6 %copy-done.1 = bf16[4,32,8192]{2,1,0:T(8,128)(2,1)S(1)} copy-done((bf16[4,32,8192]{2,1,0:T(8,128)(2,1)S(1)}, bf16[4,32,8192]{2,1,0:T(8,128)(2,1)}, u32[]{:S(2)}) %copy-start.1) | copy-done | bytes 2097176
  11.6 2.1 %collective-permute-start.7 = (bf16[640,256]{1,0:T(8,128)(2,1)S(1)}, bf16[640,256]{1,0:T(8,128)(2,1)S(1)}, u32[]{:S(2)}, u32[]{:S(2)}) collective-permute-start(bf16[640,256]{1,0:T(8,128)(2,1)S(1)} %shard_map.121.refs_4_), channel_id=1, source_target_pairs={{0,4},{4,8},{8,12},{12,16},{16,20},{20,24},{24,28},{28,0},{1,5},{5... | collective-permute-start | bytes 983048 | tf_op jit(solution)/shard_map/ppermute | solution.py:47
  13.7 1.7 %collective-permute-done.2.refs_3_ = bf16[640,256]{1,0:T(8,128)(2,1)S(1)} collective-permute-done((bf16[640,256]{1,0:T(8,128)(2,1)S(1)}, bf16[640,256]{1,0:T(8,128)(2,1)S(1)}, u32[]{:S(2)}, u32[]{:S(2)}) %collective-permute-start.2) | collective-permute-done | bytes 327712 | tf_op jit(solution)/shard_map/ppermute | solution.py:47
  15.4 1.3 %collective-permute-start.3 = (bf16[640,256]{1,0:T(8,128)(2,1)S(1)}, bf16[640,256]{1,0:T(8,128)(2,1)S(1)}, u32[]{:S(2)}, u32[]{:S(2)}) collective-permute-start(bf16[640,256]{1,0:T(8,128)(2,1)S(1)} %collective-permute-done.2.refs_3_), channel_id=1, source_target_pairs={{0,4},{4,8},{8,12},{12,16},{16,20},{20,24},{24,28},{28,0},{1,5},{5... | collective-permute-start | bytes 983048 | tf_op jit(solution)/shard_map/ppermute | solution.py:47
  17.7 1.2 %collective-permute-done.7.refs_0_ = bf16[640,256]{1,0:T(8,128)(2,1)S(1)} collective-permute-done((bf16[640,256]{1,0:T(8,128)(2,1)S(1)}, bf16[640,256]{1,0:T(8,128)(2,1)S(1)}, u32[]{:S(2)}, u32[]{:S(2)}) %collective-permute-start.7) | collective-permute-done | bytes 327712 | tf_op jit(solution)/shard_map/ppermute | solution.py:47
  18.9 1.8 %collective-permute-start.8 = (bf16[640,256]{1,0:T(8,128)(2,1)S(1)}, bf16[640,256]{1,0:T(8,128)(2,1)S(1)}, u32[]{:S(2)}, u32[]{:S(2)}) collective-permute-start(bf16[640,256]{1,0:T(8,128)(2,1)S(1)} %shard_map.123.refs_4_), channel_id=1, source_target_pairs={{0,4},{4,8},{8,12},{12,16},{16,20},{20,24},{24,28},{28,0},{1,5},{5... | collective-permute-start | bytes 983048 | tf_op jit(solution)/shard_map/ppermute | solution.py:47
  20.8 1.8 %collective-permute-done.3.refs_3_ = bf16[640,256]{1,0:T(8,128)(2,1)S(1)} collective-permute-done((bf16[640,256]{1,0:T(8,128)(2,1)S(1)}, bf16[640,256]{1,0:T(8,128)(2,1)S(1)}, u32[]{:S(2)}, u32[]{:S(2)}) %collective-permute-start.3) | collective-permute-done | bytes 327712 | tf_op jit(solution)/shard_map/ppermute | solution.py:47
  22.6 1.7 %collective-permute-start.4 = (bf16[640,256]{1,0:T(8,128)(2,1)S(1)}, bf16[640,256]{1,0:T(8,128)(2,1)S(1)}, u32[]{:S(2)}, u32[]{:S(2)}) collective-permute-start(bf16[640,256]{1,0:T(8,128)(2,1)S(1)} %collective-permute-done.3.refs_3_), channel_id=1, source_target_pairs={{0,4},{4,8},{8,12},{12,16},{16,20},{20,24},{24,28},{28,0},{1,5},{5... | collective-permute-start | bytes 983048 | tf_op jit(solution)/shard_map/ppermute | solution.py:47
  24.2 2.8 %shard_map.124 = (f32[4,256,256]{2,1,0:T(8,128)S(1)}, bf16[4,256,256]{2,1,0:T(8,128)(2,1)S(1)}, bf16[4,256,256]{2,1,0:T(8,128)(2,1)S(1)}, bf16[4,256,256]{2,1,0:T(8,128)(2,1)S(1)}, f32[8,128]{1,0:T(8,128)S(1)}) custom-call(s32[3]{0:T(128)S(1)} %pad_add_fusion.place.refs_0_, ...), custom_call_target="tpu_custom_call", output_to_operand_aliasing={{0}: (5, {}), {1}: (6, {}), {2}: (7, {}), {3}: (8, {})} | custom-call | flops 671088640 | bytes 6291456 | tf_op jit(solution)/shard_map/pallas_call | solution.py:74
  27.1 2.3 %collective-permute-start.9 = (bf16[640,256]{1,0:T(8,128)(2,1)S(1)}, bf16[640,256]{1,0:T(8,128)(2,1)S(1)}, u32[]{:S(2)}, u32[]{:S(2)}) collective-permute-start(bf16[640,256]{1,0:T(8,128)(2,1)S(1)} %shard_map.125.refs_4_), channel_id=1, source_target_pairs={{0,4},{4,8},{8,12},{12,16},{16,20},{20,24},{24,28},{28,0},{1,5},{5... | collective-permute-start | bytes 983048 | tf_op jit(solution)/shard_map/ppermute | solution.py:47
  29.4 3.4 %shard_map.126 = (f32[4,256,256]{2,1,0:T(8,128)S(1)}, bf16[4,256,256]{2,1,0:T(8,128)(2,1)S(1)}, bf16[4,256,256]{2,1,0:T(8,128)(2,1)S(1)}, bf16[4,256,256]{2,1,0:T(8,128)(2,1)S(1)}, f32[8,128]{1,0:T(8,128)}) custom-call(s32[3]{0:T(128)S(1)} %pad_add_fusion.place.refs_0_, ...), custom_call_target="tpu_custom_call", output_to_operand_aliasing={{0}: (5, {}), {1}: (6, {}), {2}: (7, {}), {3}: (8, {})} | custom-call | flops 671088640 | bytes 6291456 | tf_op jit(solution)/shard_map/pallas_call | solution.py:74
  32.9 3.6 %shard_map.127 = (f32[4,256,256]{2,1,0:T(8,128)S(1)}, bf16[4,256,256]{2,1,0:T(8,128)(2,1)S(1)}, bf16[4,256,256]{2,1,0:T(8,128)(2,1)S(1)}, bf16[4,256,256]{2,1,0:T(8,128)(2,1)S(1)}, f32[8,128]{1,0:T(8,128)}) custom-call(s32[3]{0:T(128)S(1)} %pad_add_fusion.place.refs_0_, ...), custom_call_target="tpu_custom_call", output_to_operand_aliasing={{0}: (5, {}), {1}: (6, {}), {2}: (7, {}), {3}: (8, {})} | custom-call | flops 671088640 | bytes 6291456 | tf_op jit(solution)/shard_map/pallas_call | solution.py:74
  36.5 3.4 %shard_map.128 = (f32[4,256,256]{2,1,0:T(8,128)S(1)}, bf16[4,256,256]{2,1,0:T(8,128)(2,1)S(1)}, bf16[4,256,256]{2,1,0:T(8,128)(2,1)S(1)}, bf16[4,256,256]{2,1,0:T(8,128)(2,1)S(1)}, f32[8,128]{1,0:T(8,128)}) custom-call(s32[3]{0:T(128)S(1)} %pad_add_fusion.place.refs_0_, ...), custom_call_target="tpu_custom_call", output_to_operand_aliasing={{0}: (5, {}), {1}: (6, {}), {2}: (7, {}), {3}: (8, {})} | custom-call | flops 671088640 | bytes 6291456 | tf_op jit(solution)/shard_map/pallas_call | solution.py:74
  39.9 1.3 %collective-permute-start.10 = (bf16[4,256,256]{2,1,0:T(8,128)(2,1)S(1)}, bf16[4,256,256]{2,1,0:T(8,128)(2,1)S(1)}, u32[]{:S(2)}, u32[]{:S(2)}) collective-permute-start(bf16[4,256,256]{2,1,0:T(8,128)(2,1)S(1)} %get-tuple-element.62), channel_id=1, source_target_pairs={{0,1},{4,5},{8,9},{12,13},{16,17},{20,21},{24,25},{28,29},{1,2},{5... | collective-permute-start | bytes 1572872 | tf_op jit(solution)/shard_map/ppermute | solution.py:51
  41.2 2.6 %collective-permute-start.11 = (bf16[4,256,256]{2,1,0:T(8,128)(2,1)S(1)}, bf16[4,256,256]{2,1,0:T(8,128)(2,1)S(1)}, u32[]{:S(2)}, u32[]{:S(2)}) collective-permute-start(bf16[4,256,256]{2,1,0:T(8,128)(2,1)S(1)} %get-tuple-element.63), channel_id=1, source_target_pairs={{0,2},{4,6},{8,10},{12,14},{16,18},{20,22},{24,26},{28,30},{1,3},{... | collective-permute-start | bytes 1572872 | tf_op jit(solution)/shard_map/ppermute | solution.py:51
  47.1 2.4 %collective-permute-done.10.one = bf16[4,256,256]{2,1,0:T(8,128)(2,1)S(1)} collective-permute-done((bf16[4,256,256]{2,1,0:T(8,128)(2,1)S(1)}, bf16[4,256,256]{2,1,0:T(8,128)(2,1)S(1)}, u32[]{:S(2)}, u32[]{:S(2)}) %collective-permute-start.10) | collective-permute-done | bytes 524320 | tf_op jit(solution)/shard_map/ppermute | solution.py:51
  49.5 6.8 %collective-permute-done.11.two = bf16[4,256,256]{2,1,0:T(8,128)(2,1)S(1)} collective-permute-done((bf16[4,256,256]{2,1,0:T(8,128)(2,1)S(1)}, bf16[4,256,256]{2,1,0:T(8,128)(2,1)S(1)}, u32[]{:S(2)}, u32[]{:S(2)}) %collective-permute-start.11) | collective-permute-done | bytes 524320 | tf_op jit(solution)/shard_map/ppermute | solution.py:51
  58.1 2.5 %collective-permute-start.14 = (f32[256,256]{1,0:T(8,128)S(1)}, f32[256,256]{1,0:T(8,128)S(1)}, u32[]{:S(2)}, u32[]{:S(2)}) collective-permute-start(f32[256,256]{1,0:T(8,128)S(1)} %get-tuple-element.67), channel_id=1, source_target_pairs={{0,128},{4,132},{8,136},{12,140},{16,144},{20,148},{24,152},{28,15... | collective-permute-start | bytes 786440 | tf_op jit(solution)/shard_map/ppermute | solution.py:57
  60.6 1.2 collective-permute-start.15
  61.7 5.2 %collective-permute-start.17 = (bf16[16,128,256]{2,1,0:T(8,128)(2,1)S(1)}, bf16[16,128,256]{2,1,0:T(8,128)(2,1)S(1)}, u32[]{:S(2)}, u32[]{:S(2)}) collective-permute-start(bf16[16,128,256]{2,1,0:T(8,128)(2,1)S(1)} %get-tuple-element.72), channel_id=1, source_target_pairs={{0,32},{4,36},{8,40},{12,44},{16,48},{20,52},{24,56},{28,60},{1,33... | collective-permute-start | bytes 3145736 | tf_op jit(solution)/shard_map/ppermute | solution.py:43
  67.4 9.4 %collective-permute-start.16 = (bf16[256,256]{1,0:T(8,128)(2,1)S(1)}, bf16[256,256]{1,0:T(8,128)(2,1)S(1)}, u32[]{:S(2)}, u32[]{:S(2)}) collective-permute-start(bf16[256,256]{1,0:T(8,128)(2,1)S(1)} %add_convert_fusion), channel_id=1, source_target_pairs={{0,0},{4,36},{8,72},{12,108},{16,144},{20,180},{24,216},{28,252},{... | collective-permute-start | bytes 393224 | tf_op jit(solution)/shard_map/ppermute | solution.py:63
  76.8 3.3 %collective-permute-done.16.gradient = bf16[256,256]{1,0:T(8,128)(2,1)S(1)} collective-permute-done((bf16[256,256]{1,0:T(8,128)(2,1)S(1)}, bf16[256,256]{1,0:T(8,128)(2,1)S(1)}, u32[]{:S(2)}, u32[]{:S(2)}) %collective-permute-start.16) | collective-permute-done | bytes 131104 | tf_op jit(solution)/shard_map/ppermute | solution.py:63
  83.3 3.1 %collective-permute-done.18 = bf16[256,256]{1,0:T(8,128)(2,1)S(1)} collective-permute-done((bf16[256,256]{1,0:T(8,128)(2,1)S(1)}, bf16[256,256]{1,0:T(8,128)(2,1)S(1)}, u32[]{:S(2)}, u32[]{:S(2)}) %collective-permute-start.18) | collective-permute-done | bytes 131104 | tf_op jit(solution)/shard_map/ppermute | solution.py:51
  87.2 1.3 %collective-permute-done.20 = bf16[256,256]{1,0:T(8,128)(2,1)S(1)} collective-permute-done((bf16[256,256]{1,0:T(8,128)(2,1)S(1)}, bf16[256,256]{1,0:T(8,128)(2,1)S(1)}, u32[]{:S(2)}, u32[]{:S(2)}) %collective-permute-start.20) | collective-permute-done | bytes 131104 | tf_op jit(solution)/shard_map/ppermute | solution.py:51
  88.6 2.3 %collective-permute-start.22 = (bf16[4,256,256]{2,1,0:T(8,128)(2,1)S(1)}, bf16[4,256,256]{2,1,0:T(8,128)(2,1)S(1)}, u32[]{:S(2)}, u32[]{:S(2)}) collective-permute-start(bf16[4,256,256]{2,1,0:T(8,128)(2,1)S(1)} %pad_maximum_fusion.refs_0_), channel_id=1, source_target_pairs={{0,192},{4,196},{8,200},{12,204},{16,208},{20,212},{24,216},{28,22... | collective-permute-start | bytes 1572872 | tf_op jit(solution)/shard_map/ppermute | solution.py:57
  91.0 1.5 %collective-permute-start.21 = (bf16[4,256,256]{2,1,0:T(8,128)(2,1)S(1)}, bf16[4,256,256]{2,1,0:T(8,128)(2,1)S(1)}, u32[]{:S(2)}, u32[]{:S(2)}) collective-permute-start(bf16[4,256,256]{2,1,0:T(8,128)(2,1)S(1)} %pad_maximum_fusion.refs_0_), channel_id=1, source_target_pairs={{0,128},{4,132},{8,136},{12,140},{16,144},{20,148},{24,152},{28,15... | collective-permute-start | bytes 1572872 | tf_op jit(solution)/shard_map/ppermute | solution.py:57
  92.8 9.9 %collective-permute-done.22.refs_0_ = bf16[4,256,256]{2,1,0:T(8,128)(2,1)S(1)} collective-permute-done((bf16[4,256,256]{2,1,0:T(8,128)(2,1)S(1)}, bf16[4,256,256]{2,1,0:T(8,128)(2,1)S(1)}, u32[]{:S(2)}, u32[]{:S(2)}) %collective-permute-start.22) | collective-permute-done | bytes 524320 | tf_op jit(solution)/shard_map/ppermute | solution.py:57
  102.7 3.4 %collective-permute-done.23.refs_1_ = bf16[4,256,256]{2,1,0:T(8,128)(2,1)S(1)} collective-permute-done((bf16[4,256,256]{2,1,0:T(8,128)(2,1)S(1)}, bf16[4,256,256]{2,1,0:T(8,128)(2,1)S(1)}, u32[]{:S(2)}, u32[]{:S(2)}) %collective-permute-start.23) | collective-permute-done | bytes 524320 | tf_op jit(solution)/shard_map/ppermute | solution.py:57
  106.9 11.5 %collective-permute-start.24 = (f32[128,256]{1,0:T(8,128)S(1)}, f32[128,256]{1,0:T(8,128)S(1)}, u32[]{:S(2)}, u32[]{:S(2)}) collective-permute-start(f32[128,256]{1,0:T(8,128)S(1)} %get-tuple-element.79), channel_id=1, source_target_pairs={{0,32},{4,36},{8,40},{12,44},{16,48},{20,52},{24,56},{28,60},{1,33... | collective-permute-start | bytes 393224 | tf_op jit(solution)/shard_map/ppermute | solution.py:43
  119.4 1.9 %shard_map.134 = bf16[128,1024]{1,0:T(8,128)(2,1)} custom-call(f32[128,256]{1,0:T(8,128)S(1)} %get-tuple-element.78.mine, f32[128,256]{1,0:T(8,128)S(1)} %collective-permute-done.24.theirs, bf16[128,1024]{1,0:T(8,128)(2,1)S(1)} %bitcast.51, f32[128,8]{1,0:T(8,128)S(1)} %bitcast.53, f32[128,8]{1,0:T(8,128)S(1)} %bitcast.55, f32[1024,128]{1,0:T(8,128)S(1)} %bitcast.48), custom_call_target="tpu_custom_call" | custom-call | bytes 1048576 | tf_op jit(solution)/shard_map/pallas_call | solution.py:74
  (62 shorter events, 15.6 us)
Async XLA Ops:
  0.6 16.1 %copy-start = (bf16[640,1024]{1,0:T(8,128)(2,1)S(1)}, bf16[640,1024]{1,0:T(8,128)(2,1)}, u32[]{:S(2)}) copy-start(bf16[640,1024]{1,0:T(8,128)(2,1)} %refs_1_.9) | copy-start | bytes 3932164
  0.6 16.1 %collective-permute-start = (bf16[640,1024]{1,0:T(8,128)(2,1)}, bf16[640,1024]{1,0:T(8,128)(2,1)S(1)}, u32[]{:S(2)}, u32[]{:S(2)}) collective-permute-start(bf16[640,1024]{1,0:T(8,128)(2,1)} %refs_1_.9), channel_id=1, source_target_pairs={{0,32},{4,36},{8,40},{12,44},{16,48},{20,52},{24,56},{28,60},{1,33... | collective-permute-start | bytes 3932168 | tf_op jit(solution)/shard_map/ppermute | solution.py:43
  1.4 3.3 %collective-permute-start.5 = (bf16[640,256]{1,0:T(8,128)(2,1)}, bf16[640,256]{1,0:T(8,128)(2,1)}, u32[]{:S(2)}, u32[]{:S(2)}) collective-permute-start(bf16[640,256]{1,0:T(8,128)(2,1)} %refs_3_.1), channel_id=1, source_target_pairs={{0,32},{4,36},{8,40},{12,44},{16,48},{20,52},{24,56},{28,60},{1,33... | collective-permute-start | bytes 983048 | tf_op jit(solution)/shard_map/ppermute | solution.py:43
  1.5 6.6 %collective-permute-start.1 = (bf16[640,256]{1,0:T(8,128)(2,1)}, bf16[640,256]{1,0:T(8,128)(2,1)S(1)}, u32[]{:S(2)}, u32[]{:S(2)}) collective-permute-start(bf16[640,256]{1,0:T(8,128)(2,1)} %refs_3_.1), channel_id=1, source_target_pairs={{0,4},{4,8},{8,12},{12,16},{16,20},{20,24},{24,28},{28,0},{1,5},{5... | collective-permute-start | bytes 983048 | tf_op jit(solution)/shard_map/ppermute | solution.py:47
  4.7 6.9 %collective-permute-start.6 = (bf16[640,256]{1,0:T(8,128)(2,1)}, bf16[640,256]{1,0:T(8,128)(2,1)S(1)}, u32[]{:S(2)}, u32[]{:S(2)}) collective-permute-start(bf16[640,256]{1,0:T(8,128)(2,1)} %collective-permute-done.5.refs_4_), channel_id=1, source_target_pairs={{0,4},{4,8},{8,12},{12,16},{16,20},{20,24},{24,28},{28,0},{1,5},{5... | collective-permute-start | bytes 983048 | tf_op jit(solution)/shard_map/ppermute | solution.py:47
  8.1 7.3 %collective-permute-start.2 = (bf16[640,256]{1,0:T(8,128)(2,1)S(1)}, bf16[640,256]{1,0:T(8,128)(2,1)S(1)}, u32[]{:S(2)}, u32[]{:S(2)}) collective-permute-start(bf16[640,256]{1,0:T(8,128)(2,1)S(1)} %collective-permute-done.1.refs_3_), channel_id=1, source_target_pairs={{0,4},{4,8},{8,12},{12,16},{16,20},{20,24},{24,28},{28,0},{1,5},{5... | collective-permute-start | bytes 983048 | tf_op jit(solution)/shard_map/ppermute | solution.py:47
  9.8 6.9 %copy-start.3 = (bf16[640,256]{1,0:T(8,128)(2,1)S(1)}, bf16[640,256]{1,0:T(8,128)(2,1)}, u32[]{:S(2)}) copy-start(bf16[640,256]{1,0:T(8,128)(2,1)} %refs_3_.1) | copy-start | bytes 983044
  11.6 9.1 %copy-start.2 = (bf16[4,32,1024]{2,1,0:T(8,128)(2,1)S(1)}, bf16[4,32,1024]{2,1,0:T(8,128)(2,1)}, u32[]{:S(2)}) copy-start(bf16[4,32,1024]{2,1,0:T(8,128)(2,1)} %param.15) | copy-start | bytes 786436
  11.6 7.3 %collective-permute-start.7 = (bf16[640,256]{1,0:T(8,128)(2,1)S(1)}, bf16[640,256]{1,0:T(8,128)(2,1)S(1)}, u32[]{:S(2)}, u32[]{:S(2)}) collective-permute-start(bf16[640,256]{1,0:T(8,128)(2,1)S(1)} %shard_map.121.refs_4_), channel_id=1, source_target_pairs={{0,4},{4,8},{8,12},{12,16},{16,20},{20,24},{24,28},{28,0},{1,5},{5... | collective-permute-start | bytes 983048 | tf_op jit(solution)/shard_map/ppermute | solution.py:47
  15.4 7.1 %collective-permute-start.3 = (bf16[640,256]{1,0:T(8,128)(2,1)S(1)}, bf16[640,256]{1,0:T(8,128)(2,1)S(1)}, u32[]{:S(2)}, u32[]{:S(2)}) collective-permute-start(bf16[640,256]{1,0:T(8,128)(2,1)S(1)} %collective-permute-done.2.refs_3_), channel_id=1, source_target_pairs={{0,4},{4,8},{8,12},{12,16},{16,20},{20,24},{24,28},{28,0},{1,5},{5... | collective-permute-start | bytes 983048 | tf_op jit(solution)/shard_map/ppermute | solution.py:47
  18.9 8.1 %collective-permute-start.8 = (bf16[640,256]{1,0:T(8,128)(2,1)S(1)}, bf16[640,256]{1,0:T(8,128)(2,1)S(1)}, u32[]{:S(2)}, u32[]{:S(2)}) collective-permute-start(bf16[640,256]{1,0:T(8,128)(2,1)S(1)} %shard_map.123.refs_4_), channel_id=1, source_target_pairs={{0,4},{4,8},{8,12},{12,16},{16,20},{20,24},{24,28},{28,0},{1,5},{5... | collective-permute-start | bytes 983048 | tf_op jit(solution)/shard_map/ppermute | solution.py:47
  22.6 13.9 %collective-permute-start.4 = (bf16[640,256]{1,0:T(8,128)(2,1)S(1)}, bf16[640,256]{1,0:T(8,128)(2,1)S(1)}, u32[]{:S(2)}, u32[]{:S(2)}) collective-permute-start(bf16[640,256]{1,0:T(8,128)(2,1)S(1)} %collective-permute-done.3.refs_3_), channel_id=1, source_target_pairs={{0,4},{4,8},{8,12},{12,16},{16,20},{20,24},{24,28},{28,0},{1,5},{5... | collective-permute-start | bytes 983048 | tf_op jit(solution)/shard_map/ppermute | solution.py:47
  27.1 9.4 %collective-permute-start.9 = (bf16[640,256]{1,0:T(8,128)(2,1)S(1)}, bf16[640,256]{1,0:T(8,128)(2,1)S(1)}, u32[]{:S(2)}, u32[]{:S(2)}) collective-permute-start(bf16[640,256]{1,0:T(8,128)(2,1)S(1)} %shard_map.125.refs_4_), channel_id=1, source_target_pairs={{0,4},{4,8},{8,12},{12,16},{16,20},{20,24},{24,28},{28,0},{1,5},{5... | collective-permute-start | bytes 983048 | tf_op jit(solution)/shard_map/ppermute | solution.py:47
  36.5 8.4 %copy-start.7 = (bf16[32,256,256]{2,1,0:T(8,128)(2,1)S(1)}, bf16[32,256,256]{2,1,0:T(8,128)(2,1)}, u32[]{:S(2)}) copy-start(bf16[32,256,256]{2,1,0:T(8,128)(2,1)} %param.16) | copy-start | bytes 12582916
  39.9 9.6 %collective-permute-start.10 = (bf16[4,256,256]{2,1,0:T(8,128)(2,1)S(1)}, bf16[4,256,256]{2,1,0:T(8,128)(2,1)S(1)}, u32[]{:S(2)}, u32[]{:S(2)}) collective-permute-start(bf16[4,256,256]{2,1,0:T(8,128)(2,1)S(1)} %get-tuple-element.62), channel_id=1, source_target_pairs={{0,1},{4,5},{8,9},{12,13},{16,17},{20,21},{24,25},{28,29},{1,2},{5... | collective-permute-start | bytes 1572872 | tf_op jit(solution)/shard_map/ppermute | solution.py:51
  41.2 15.1 %collective-permute-start.11 = (bf16[4,256,256]{2,1,0:T(8,128)(2,1)S(1)}, bf16[4,256,256]{2,1,0:T(8,128)(2,1)S(1)}, u32[]{:S(2)}, u32[]{:S(2)}) collective-permute-start(bf16[4,256,256]{2,1,0:T(8,128)(2,1)S(1)} %get-tuple-element.63), channel_id=1, source_target_pairs={{0,2},{4,6},{8,10},{12,14},{16,18},{20,22},{24,26},{28,30},{1,3},{... | collective-permute-start | bytes 1572872 | tf_op jit(solution)/shard_map/ppermute | solution.py:51
  43.8 12.5 %collective-permute-start.12 = (bf16[4,256,256]{2,1,0:T(8,128)(2,1)S(1)}, bf16[4,256,256]{2,1,0:T(8,128)(2,1)S(1)}, u32[]{:S(2)}, u32[]{:S(2)}) collective-permute-start(bf16[4,256,256]{2,1,0:T(8,128)(2,1)S(1)} %get-tuple-element.64), channel_id=1, source_target_pairs={{0,3},{4,7},{8,11},{12,15},{16,19},{20,23},{24,27},{28,31},{1,0},{... | collective-permute-start | bytes 1572872 | tf_op jit(solution)/shard_map/ppermute | solution.py:51
  56.3 23.8 %copy-start.4 = (f32[256,256]{1,0:T(8,128)S(1)}, f32[256,256]{1,0:T(8,128)}, u32[]{:S(2)}) copy-start(f32[256,256]{1,0:T(8,128)} %master.1) | copy-start | bytes 786436
  56.3 23.8 %copy-start.5 = (bf16[256,256]{1,0:T(8,128)(2,1)S(1)}, bf16[256,256]{1,0:T(8,128)(2,1)}, u32[]{:S(2)}) copy-start(bf16[256,256]{1,0:T(8,128)(2,1)} %first_moment.1) | copy-start | bytes 393220
  56.3 23.8 %copy-start.6 = (bf16[256,256]{1,0:T(8,128)(2,1)S(1)}, bf16[256,256]{1,0:T(8,128)(2,1)}, u32[]{:S(2)}) copy-start(bf16[256,256]{1,0:T(8,128)(2,1)} %second_moment.1) | copy-start | bytes 393220
  57.1 9.8 %collective-permute-start.13 = (f32[256,256]{1,0:T(8,128)S(1)}, f32[256,256]{1,0:T(8,128)S(1)}, u32[]{:S(2)}, u32[]{:S(2)}) collective-permute-start(f32[256,256]{1,0:T(8,128)S(1)} %get-tuple-element.66), channel_id=1, source_target_pairs={{0,64},{4,68},{8,72},{12,76},{16,80},{20,84},{24,88},{28,92},{1,65... | collective-permute-start | bytes 786440 | tf_op jit(solution)/shard_map/ppermute | solution.py:57
  58.1 9.0 %collective-permute-start.14 = (f32[256,256]{1,0:T(8,128)S(1)}, f32[256,256]{1,0:T(8,128)S(1)}, u32[]{:S(2)}, u32[]{:S(2)}) collective-permute-start(f32[256,256]{1,0:T(8,128)S(1)} %get-tuple-element.67), channel_id=1, source_target_pairs={{0,128},{4,132},{8,136},{12,140},{16,144},{20,148},{24,152},{28,15... | collective-permute-start | bytes 786440 | tf_op jit(solution)/shard_map/ppermute | solution.py:57
  60.6 6.7 %collective-permute-start.15 = (f32[256,256]{1,0:T(8,128)S(1)}, f32[256,256]{1,0:T(8,128)S(1)}, u32[]{:S(2)}, u32[]{:S(2)}) collective-permute-start(f32[256,256]{1,0:T(8,128)S(1)} %get-tuple-element.68), channel_id=1, source_target_pairs={{0,192},{4,196},{8,200},{12,204},{16,208},{20,212},{24,216},{28,22... | collective-permute-start | bytes 786440 | tf_op jit(solution)/shard_map/ppermute | solution.py:57
  61.7 30.7 %collective-permute-start.17 = (bf16[16,128,256]{2,1,0:T(8,128)(2,1)S(1)}, bf16[16,128,256]{2,1,0:T(8,128)(2,1)S(1)}, u32[]{:S(2)}, u32[]{:S(2)}) collective-permute-start(bf16[16,128,256]{2,1,0:T(8,128)(2,1)S(1)} %get-tuple-element.72), channel_id=1, source_target_pairs={{0,32},{4,36},{8,40},{12,44},{16,48},{20,52},{24,56},{28,60},{1,33... | collective-permute-start | bytes 3145736 | tf_op jit(solution)/shard_map/ppermute | solution.py:43
  67.4 12.7 %collective-permute-start.16 = (bf16[256,256]{1,0:T(8,128)(2,1)S(1)}, bf16[256,256]{1,0:T(8,128)(2,1)S(1)}, u32[]{:S(2)}, u32[]{:S(2)}) collective-permute-start(bf16[256,256]{1,0:T(8,128)(2,1)S(1)} %add_convert_fusion), channel_id=1, source_target_pairs={{0,0},{4,36},{8,72},{12,108},{16,144},{20,180},{24,216},{28,252},{... | collective-permute-start | bytes 393224 | tf_op jit(solution)/shard_map/ppermute | solution.py:63
  81.2 5.2 %collective-permute-start.18 = (bf16[256,256]{1,0:T(8,128)(2,1)S(1)}, bf16[256,256]{1,0:T(8,128)(2,1)S(1)}, u32[]{:S(2)}, u32[]{:S(2)}) collective-permute-start(bf16[256,256]{1,0:T(8,128)(2,1)S(1)} %get-tuple-element.73), channel_id=1, source_target_pairs={{0,3},{4,7},{8,11},{12,15},{16,19},{20,23},{24,27},{28,31},{1,0},{... | collective-permute-start | bytes 393224 | tf_op jit(solution)/shard_map/ppermute | solution.py:51
  81.8 5.4 %collective-permute-start.19 = (bf16[256,256]{1,0:T(8,128)(2,1)S(1)}, bf16[256,256]{1,0:T(8,128)(2,1)S(1)}, u32[]{:S(2)}, u32[]{:S(2)}) collective-permute-start(bf16[256,256]{1,0:T(8,128)(2,1)S(1)} %get-tuple-element.73), channel_id=1, source_target_pairs={{0,2},{4,6},{8,10},{12,14},{16,18},{20,22},{24,26},{28,30},{1,3},{... | collective-permute-start | bytes 393224 | tf_op jit(solution)/shard_map/ppermute | solution.py:51
  82.5 6.1 %collective-permute-start.20 = (bf16[256,256]{1,0:T(8,128)(2,1)S(1)}, bf16[256,256]{1,0:T(8,128)(2,1)S(1)}, u32[]{:S(2)}, u32[]{:S(2)}) collective-permute-start(bf16[256,256]{1,0:T(8,128)(2,1)S(1)} %get-tuple-element.73), channel_id=1, source_target_pairs={{0,1},{4,5},{8,9},{12,13},{16,17},{20,21},{24,25},{28,29},{1,2},{5... | collective-permute-start | bytes 393224 | tf_op jit(solution)/shard_map/ppermute | solution.py:51
  88.6 14.1 %collective-permute-start.22 = (bf16[4,256,256]{2,1,0:T(8,128)(2,1)S(1)}, bf16[4,256,256]{2,1,0:T(8,128)(2,1)S(1)}, u32[]{:S(2)}, u32[]{:S(2)}) collective-permute-start(bf16[4,256,256]{2,1,0:T(8,128)(2,1)S(1)} %pad_maximum_fusion.refs_0_), channel_id=1, source_target_pairs={{0,192},{4,196},{8,200},{12,204},{16,208},{20,212},{24,216},{28,22... | collective-permute-start | bytes 1572872 | tf_op jit(solution)/shard_map/ppermute | solution.py:57
  90.9 15.2 %collective-permute-start.23 = (bf16[4,256,256]{2,1,0:T(8,128)(2,1)S(1)}, bf16[4,256,256]{2,1,0:T(8,128)(2,1)S(1)}, u32[]{:S(2)}, u32[]{:S(2)}) collective-permute-start(bf16[4,256,256]{2,1,0:T(8,128)(2,1)S(1)} %pad_maximum_fusion.refs_0_), channel_id=1, source_target_pairs={{0,64},{4,68},{8,72},{12,76},{16,80},{20,84},{24,88},{28,92},{1,65... | collective-permute-start | bytes 1572872 | tf_op jit(solution)/shard_map/ppermute | solution.py:57
  91.0 15.6 %collective-permute-start.21 = (bf16[4,256,256]{2,1,0:T(8,128)(2,1)S(1)}, bf16[4,256,256]{2,1,0:T(8,128)(2,1)S(1)}, u32[]{:S(2)}, u32[]{:S(2)}) collective-permute-start(bf16[4,256,256]{2,1,0:T(8,128)(2,1)S(1)} %pad_maximum_fusion.refs_0_), channel_id=1, source_target_pairs={{0,128},{4,132},{8,136},{12,140},{16,144},{20,148},{24,152},{28,15... | collective-permute-start | bytes 1572872 | tf_op jit(solution)/shard_map/ppermute | solution.py:57
  106.9 12.5 %collective-permute-start.24 = (f32[128,256]{1,0:T(8,128)S(1)}, f32[128,256]{1,0:T(8,128)S(1)}, u32[]{:S(2)}, u32[]{:S(2)}) collective-permute-start(f32[128,256]{1,0:T(8,128)S(1)} %get-tuple-element.79), channel_id=1, source_target_pairs={{0,32},{4,36},{8,40},{12,44},{16,48},{20,52},{24,56},{28,60},{1,33... | collective-permute-start | bytes 393224 | tf_op jit(solution)/shard_map/ppermute | solution.py:43
  (2 other events, 6.7 us)

commit v2 on v1

--- a/solution.py
+++ b/solution.py
@@ -105,28 +105,32 @@
     place, own_x, other_x, block, other_block = refs[:5]
     keep, one, two, three, token = refs[5:] if first else refs[9:]
     k, p = place[0], place[1]
-    slot = jnp.where(k == 0, step, 4 - step)
+    sends = (keep, one, two, three)
     token[...] = jnp.zeros_like(token)
 
-    @pl.when((slot >= 0) & (slot < 4))
-    def _():
-        mine, theirs = block[...].T, other_block[...].T
-        for a in range(4):
-            at = slice(a * 256, a * 256 + 256)
-            tile = jnp.dot(mine, own_x[:, at], preferred_element_type=f32)
-            tile = tile + jnp.dot(theirs, other_x[:, at], preferred_element_type=f32)
-            d = lax.rem(jnp.where(k == 0, a, slot) - p + 4, 4)
-            index = jnp.where(k == 0, slot, a)
-
-            @pl.when(d == 0)
+    def tile(mine, theirs, a):
+        at = pl.ds(pl.multiple_of(a * 256, 256), 256)
+        return jnp.dot(mine, own_x[:, at], preferred_element_type=f32) + jnp.dot(
+            theirs, other_x[:, at], preferred_element_type=f32
+        )
+
+    if step < 4:
+
+        @pl.when(k == 0)
+        def _():
+            mine, theirs = block[...].T, other_block[...].T
+            for d, out in enumerate(sends):
+                out[step] = tile(mine, theirs, lax.rem(p + d, 4)).astype(out.dtype)
+
+    if step > 0:
+        slot = 4 - step
+        for d, out in enumerate(sends):
+
+            @pl.when((k == 1) & (lax.rem(p + d, 4) == slot))
             def _():
-                keep[index] = tile
-
-            for m, out in ((1, one), (2, two), (3, three)):
-
-                @pl.when(d == m)
-                def _():
-                    out[index] = tile.astype(bf16)
+                mine, theirs = block[...].T, other_block[...].T
+                for a in range(4):
+                    out[a] = tile(mine, theirs, a).astype(out.dtype)
 
 
 def middle_kernel(place, keep, one, two, three, *refs):
@@ -290,12 +294,9 @@
     tokens = []
     arrived = (block, other_block)
     for step in range(5):
-        if step == 1:
-            arrived = (arrived[0], after_all(arrived[1], kept))
-        if step == 2:
-            arrived = (arrived[0], after_all(arrived[1], tokens[0]))
-        if step == 3:
-            arrived = (arrived[0], after_all(arrived[1], tokens[1]))
+        if 0 < step < 4:
+            awaited = (tokens[-1], kept) if step == 1 else (tokens[-1],)
+            arrived = (arrived[0], after_all(arrived[1], *awaited))
         if step < 4:
             after = (pass_on(arrived[0]), pass_on(arrived[1]))
         buffers, token = add_slot(step, *arrived, buffers)

time: 121 us -> 121 us (level)
  the two profiles are of different devices: /device:TPU:65 before, /device:TPU:32 now
where the time goes in v2:
time: 121 us; the launch traced here: 118 us
  waiting for transfers between devices  51 us (42%)
  starting transfers between devices  48.1 us (40%)
  Pallas kernels  14.3 us (12%)
  local copies, waits for them, and re-layouts  1.99 us (2%)
  matrix products  1.35 us (1%)
    ppermute x6, starting transfers between devices, shift_second(): lax.ppermute(a, AXES, pairs_of(lambda y, k, x, z: (y + d, k, x, z) if k =...  19.5 us
    ppermute x6, waiting for transfers between devices, shift_second(): lax.ppermute(a, AXES, pairs_of(lambda y, k, x, z: (y + d, k, x, z) if k =...  17.8 us
    ppermute x8, starting transfers between devices, pass_on(): lax.ppermute(a, AXES, pairs_of(lambda y, k, x, z: (y, k, x, z + 1 - 2 * k)))  16 us
    ppermute x6, waiting for transfers between devices, shift_first(): lax.ppermute(a, AXES, pairs_of(lambda y, k, x, z: (y, k, x + d, z) if k =...  15.2 us
    pallas_call x15, Pallas kernels, call(): pl.pallas_call(kernel, out_shape=out, in_specs=in_specs, out_specs=out_sp...  14.3 us
    ppermute x6, starting transfers between devices, shift_first(): lax.ppermute(a, AXES, pairs_of(lambda y, k, x, z: (y, k, x + d, z) if k =...  10 us
    ppermute x8, waiting for transfers between devices, pass_on(): lax.ppermute(a, AXES, pairs_of(lambda y, k, x, z: (y, k, x, z + 1 - 2 * k)))  9.12 us
    ppermute x1, waiting for transfers between devices, to_owner(): lax.ppermute(a, AXES, pairs_of(lambda y, k, x, z: (z // 2, z % 2, x, z +...  6.47 us
  transfers between devices with their start and end apart: 25, of which 18 were waited for; matrix products, arithmetic and copies ran while one was open for 2% of the time, Pallas kernels for 9%

profile of v2, /device:TPU:32, one launch (start us, length us, event | category | flops | bytes accessed | tf_op | source)
XLA Modules:
  0.0 118.3 jit_solution(15719193298630781012)
XLA Ops:
  1.2 1.9 %collective-permute-start.1 = (bf16[640,256]{1,0:T(8,128)(2,1)}, bf16[640,256]{1,0:T(8,128)(2,1)S(1)}, u32[]{:S(2)}, u32[]{:S(2)}) collective-permute-start(bf16[640,256]{1,0:T(8,128)(2,1)} %refs_3_.1), channel_id=1, source_target_pairs={{0,4},{4,8},{8,12},{12,16},{16,20},{20,24},{24,28},{28,0},{1,5},{5... | collective-permute-start | bytes 983048 | tf_op jit(solution)/shard_map/ppermute | solution.py:47
  4.2 1.9 %collective-permute-start.6 = (bf16[640,256]{1,0:T(8,128)(2,1)}, bf16[640,256]{1,0:T(8,128)(2,1)S(1)}, u32[]{:S(2)}, u32[]{:S(2)}) collective-permute-start(bf16[640,256]{1,0:T(8,128)(2,1)} %collective-permute-done.5.refs_4_), channel_id=1, source_target_pairs={{0,4},{4,8},{8,12},{12,16},{16,20},{20,24},{24,28},{28,0},{1,5},{5... | collective-permute-start | bytes 983048 | tf_op jit(solution)/shard_map/ppermute | solution.py:47
  6.2 1.6 %copy-done.1 = bf16[4,32,8192]{2,1,0:T(8,128)(2,1)S(1)} copy-done((bf16[4,32,8192]{2,1,0:T(8,128)(2,1)S(1)}, bf16[4,32,8192]{2,1,0:T(8,128)(2,1)}, u32[]{:S(2)}) %copy-start.1) | copy-done | bytes 2097176
  8.6 2.2 %collective-permute-start.2 = (bf16[640,256]{1,0:T(8,128)(2,1)S(1)}, bf16[640,256]{1,0:T(8,128)(2,1)S(1)}, u32[]{:S(2)}, u32[]{:S(2)}) collective-permute-start(bf16[640,256]{1,0:T(8,128)(2,1)S(1)} %collective-permute-done.1.refs_3_), channel_id=1, source_target_pairs={{0,4},{4,8},{8,12},{12,16},{16,20},{20,24},{24,28},{28,0},{1,5},{5... | collective-permute-start | bytes 983048 | tf_op jit(solution)/shard_map/ppermute | solution.py:47
  10.8 2.0 %shard_map.120 = (f32[4,256,256]{2,1,0:T(8,128)S(1)}, bf16[4,256,256]{2,1,0:T(8,128)(2,1)S(1)}, bf16[4,256,256]{2,1,0:T(8,128)(2,1)S(1)}, bf16[4,256,256]{2,1,0:T(8,128)(2,1)S(1)}, f32[8,128]{1,0:T(8,128)S(1)}) custom-call(s32[3]{0:T(128)S(1)} %pad_add_fusion.refs_0_.place, bf16[640,1024]{1,0:T(8,128)(2,1)S(1)} %copy-done, ...), custom_call_target="tpu_custom_call" | custom-call | flops 671088640 | bytes 6291456 | tf_op jit(solution)/shard_map/pallas_call | solution.py:74
  12.8 3.0 %collective-permute-start.7 = (bf16[640,256]{1,0:T(8,128)(2,1)S(1)}, bf16[640,256]{1,0:T(8,128)(2,1)S(1)}, u32[]{:S(2)}, u32[]{:S(2)}) collective-permute-start(bf16[640,256]{1,0:T(8,128)(2,1)S(1)} %shard_map.122.refs_4_), channel_id=1, source_target_pairs={{0,4},{4,8},{8,12},{12,16},{16,20},{20,24},{24,28},{28,0},{1,5},{5... | collective-permute-start | bytes 983048 | tf_op jit(solution)/shard_map/ppermute | solution.py:47
  15.9 1.6 %collective-permute-done.2.refs_3_ = bf16[640,256]{1,0:T(8,128)(2,1)S(1)} collective-permute-done((bf16[640,256]{1,0:T(8,128)(2,1)S(1)}, bf16[640,256]{1,0:T(8,128)(2,1)S(1)}, u32[]{:S(2)}, u32[]{:S(2)}) %collective-permute-start.2) | collective-permute-done | bytes 327712 | tf_op jit(solution)/shard_map/ppermute | solution.py:47
  18.8 1.6 %shard_map.123 = (f32[4,256,256]{2,1,0:T(8,128)S(1)}, bf16[4,256,256]{2,1,0:T(8,128)(2,1)S(1)}, bf16[4,256,256]{2,1,0:T(8,128)(2,1)S(1)}, bf16[4,256,256]{2,1,0:T(8,128)(2,1)S(1)}, f32[8,128]{1,0:T(8,128)S(1)}) custom-call(s32[3]{0:T(128)S(1)} %pad_add_fusion.refs_0_.place, ...), custom_call_target="tpu_custom_call", output_to_operand_aliasing={{0}: (5, {}), {1}: (6, {}), {2}: (7, {}), {3}: (8, {})} | custom-call | flops 671088640 | bytes 6291456 | tf_op jit(solution)/shard_map/pallas_call | solution.py:74
  21.0 2.4 %collective-permute-start.8 = (bf16[640,256]{1,0:T(8,128)(2,1)S(1)}, bf16[640,256]{1,0:T(8,128)(2,1)S(1)}, u32[]{:S(2)}, u32[]{:S(2)}) collective-permute-start(bf16[640,256]{1,0:T(8,128)(2,1)S(1)} %shard_map.124.refs_4_), channel_id=1, source_target_pairs={{0,4},{4,8},{8,12},{12,16},{16,20},{20,24},{24,28},{28,0},{1,5},{5... | collective-permute-start | bytes 983048 | tf_op jit(solution)/shard_map/ppermute | solution.py:47
  23.4 2.4 %collective-permute-done.3.refs_3_ = bf16[640,256]{1,0:T(8,128)(2,1)S(1)} collective-permute-done((bf16[640,256]{1,0:T(8,128)(2,1)S(1)}, bf16[640,256]{1,0:T(8,128)(2,1)S(1)}, u32[]{:S(2)}, u32[]{:S(2)}) %collective-permute-start.3) | collective-permute-done | bytes 327712 | tf_op jit(solution)/shard_map/ppermute | solution.py:47
  26.9 1.8 %shard_map.125 = (f32[4,256,256]{2,1,0:T(8,128)S(1)}, bf16[4,256,256]{2,1,0:T(8,128)(2,1)S(1)}, bf16[4,256,256]{2,1,0:T(8,128)(2,1)S(1)}, bf16[4,256,256]{2,1,0:T(8,128)(2,1)S(1)}, f32[8,128]{1,0:T(8,128)S(1)}) custom-call(s32[3]{0:T(128)S(1)} %pad_add_fusion.refs_0_.place, ...), custom_call_target="tpu_custom_call", output_to_operand_aliasing={{0}: (5, {}), {1}: (6, {}), {2}: (7, {}), {3}: (8, {})} | custom-call | flops 671088640 | bytes 6291456 | tf_op jit(solution)/shard_map/pallas_call | solution.py:74
  29.3 2.1 %collective-permute-start.9 = (bf16[640,256]{1,0:T(8,128)(2,1)S(1)}, bf16[640,256]{1,0:T(8,128)(2,1)S(1)}, u32[]{:S(2)}, u32[]{:S(2)}) collective-permute-start(bf16[640,256]{1,0:T(8,128)(2,1)S(1)} %shard_map.126.refs_4_), channel_id=1, source_target_pairs={{0,4},{4,8},{8,12},{12,16},{16,20},{20,24},{24,28},{28,0},{1,5},{5... | collective-permute-start | bytes 983048 | tf_op jit(solution)/shard_map/ppermute | solution.py:47
  31.6 2.2 %shard_map.127 = (f32[4,256,256]{2,1,0:T(8,128)S(1)}, bf16[4,256,256]{2,1,0:T(8,128)(2,1)S(1)}, bf16[4,256,256]{2,1,0:T(8,128)(2,1)S(1)}, bf16[4,256,256]{2,1,0:T(8,128)(2,1)S(1)}, f32[8,128]{1,0:T(8,128)}) custom-call(s32[3]{0:T(128)S(1)} %pad_add_fusion.refs_0_.place, ...), custom_call_target="tpu_custom_call", output_to_operand_aliasing={{0}: (5, {}), {1}: (6, {}), {2}: (7, {}), {3}: (8, {})} | custom-call | flops 671088640 | bytes 6291456 | tf_op jit(solution)/shard_map/pallas_call | solution.py:74
  34.1 3.5 %collective-permute-done.9.refs_4_ = bf16[640,256]{1,0:T(8,128)(2,1)S(1)} collective-permute-done((bf16[640,256]{1,0:T(8,128)(2,1)S(1)}, bf16[640,256]{1,0:T(8,128)(2,1)S(1)}, u32[]{:S(2)}, u32[]{:S(2)}) %collective-permute-start.9) | collective-permute-done | bytes 327712 | tf_op jit(solution)/shard_map/ppermute | solution.py:47
  38.8 1.5 %collective-permute-start.10 = (bf16[4,256,256]{2,1,0:T(8,128)(2,1)S(1)}, bf16[4,256,256]{2,1,0:T(8,128)(2,1)S(1)}, u32[]{:S(2)}, u32[]{:S(2)}) collective-permute-start(bf16[4,256,256]{2,1,0:T(8,128)(2,1)S(1)} %get-tuple-element.64), channel_id=1, source_target_pairs={{0,1},{4,5},{8,9},{12,13},{16,17},{20,21},{24,25},{28,29},{1,2},{5... | collective-permute-start | bytes 1572872 | tf_op jit(solution)/shard_map/ppermute | solution.py:51
  40.3 2.7 %collective-permute-start.11 = (bf16[4,256,256]{2,1,0:T(8,128)(2,1)S(1)}, bf16[4,256,256]{2,1,0:T(8,128)(2,1)S(1)}, u32[]{:S(2)}, u32[]{:S(2)}) collective-permute-start(bf16[4,256,256]{2,1,0:T(8,128)(2,1)S(1)} %get-tuple-element.65), channel_id=1, source_target_pairs={{0,2},{4,6},{8,10},{12,14},{16,18},{20,22},{24,26},{28,30},{1,3},{... | collective-permute-start | bytes 1572872 | tf_op jit(solution)/shard_map/ppermute | solution.py:51
  43.0 1.4 %collective-permute-start.12 = (bf16[4,256,256]{2,1,0:T(8,128)(2,1)S(1)}, bf16[4,256,256]{2,1,0:T(8,128)(2,1)S(1)}, u32[]{:S(2)}, u32[]{:S(2)}) collective-permute-start(bf16[4,256,256]{2,1,0:T(8,128)(2,1)S(1)} %get-tuple-element.66), channel_id=1, source_target_pairs={{0,3},{4,7},{8,11},{12,15},{16,19},{20,23},{24,27},{28,31},{1,0},{... | collective-permute-start | bytes 1572872 | tf_op jit(solution)/shard_map/ppermute | solution.py:51
  46.6 2.6 %collective-permute-done.10.one = bf16[4,256,256]{2,1,0:T(8,128)(2,1)S(1)} collective-permute-done((bf16[4,256,256]{2,1,0:T(8,128)(2,1)S(1)}, bf16[4,256,256]{2,1,0:T(8,128)(2,1)S(1)}, u32[]{:S(2)}, u32[]{:S(2)}) %collective-permute-start.10) | collective-permute-done | bytes 524320 | tf_op jit(solution)/shard_map/ppermute | solution.py:51
  49.2 6.6 %collective-permute-done.11.two = bf16[4,256,256]{2,1,0:T(8,128)(2,1)S(1)} collective-permute-done((bf16[4,256,256]{2,1,0:T(8,128)(2,1)S(1)}, bf16[4,256,256]{2,1,0:T(8,128)(2,1)S(1)}, u32[]{:S(2)}, u32[]{:S(2)}) %collective-permute-start.11) | collective-permute-done | bytes 524320 | tf_op jit(solution)/shard_map/ppermute | solution.py:51
  56.6 1.7 %collective-permute-start.13 = (f32[256,256]{1,0:T(8,128)S(1)}, f32[256,256]{1,0:T(8,128)S(1)}, u32[]{:S(2)}, u32[]{:S(2)}) collective-permute-start(f32[256,256]{1,0:T(8,128)S(1)} %get-tuple-element.68), channel_id=1, source_target_pairs={{0,64},{4,68},{8,72},{12,76},{16,80},{20,84},{24,88},{28,92},{1,65... | collective-permute-start | bytes 786440 | tf_op jit(solution)/shard_map/ppermute | solution.py:57
  58.2 2.9 %collective-permute-start.14 = (f32[256,256]{1,0:T(8,128)S(1)}, f32[256,256]{1,0:T(8,128)S(1)}, u32[]{:S(2)}, u32[]{:S(2)}) collective-permute-start(f32[256,256]{1,0:T(8,128)S(1)} %get-tuple-element.69), channel_id=1, source_target_pairs={{0,128},{4,132},{8,136},{12,140},{16,144},{20,148},{24,152},{28,15... | collective-permute-start | bytes 786440 | tf_op jit(solution)/shard_map/ppermute | solution.py:57
  62.5 1.8 %collective-permute-done.13 = f32[256,256]{1,0:T(8,128)S(1)} collective-permute-done((f32[256,256]{1,0:T(8,128)S(1)}, f32[256,256]{1,0:T(8,128)S(1)}, u32[]{:S(2)}, u32[]{:S(2)}) %collective-permute-start.13) | collective-permute-done | bytes 262176 | tf_op jit(solution)/shard_map/ppermute | solution.py:57
  64.2 4.0 %collective-permute-done.14 = f32[256,256]{1,0:T(8,128)S(1)} collective-permute-done((f32[256,256]{1,0:T(8,128)S(1)}, f32[256,256]{1,0:T(8,128)S(1)}, u32[]{:S(2)}, u32[]{:S(2)}) %collective-permute-start.14) | collective-permute-done | bytes 262176 | tf_op jit(solution)/shard_map/ppermute | solution.py:57
  68.4 1.9 %collective-permute-start.16 = (bf16[256,256]{1,0:T(8,128)(2,1)S(1)}, bf16[256,256]{1,0:T(8,128)(2,1)S(1)}, u32[]{:S(2)}, u32[]{:S(2)}) collective-permute-start(bf16[256,256]{1,0:T(8,128)(2,1)S(1)} %add_convert_fusion), channel_id=1, source_target_pairs={{0,0},{4,36},{8,72},{12,108},{16,144},{20,180},{24,216},{28,252},{... | collective-permute-start | bytes 393224 | tf_op jit(solution)/shard_map/ppermute | solution.py:63
  70.3 6.5 %collective-permute-done.16.gradient = bf16[256,256]{1,0:T(8,128)(2,1)S(1)} collective-permute-done((bf16[256,256]{1,0:T(8,128)(2,1)S(1)}, bf16[256,256]{1,0:T(8,128)(2,1)S(1)}, u32[]{:S(2)}, u32[]{:S(2)}) %collective-permute-start.16) | collective-permute-done | bytes 131104 | tf_op jit(solution)/shard_map/ppermute | solution.py:63
  77.9 2.5 %collective-permute-start.18 = (bf16[256,256]{1,0:T(8,128)(2,1)S(1)}, bf16[256,256]{1,0:T(8,128)(2,1)S(1)}, u32[]{:S(2)}, u32[]{:S(2)}) collective-permute-start(bf16[256,256]{1,0:T(8,128)(2,1)S(1)} %get-tuple-element.75), channel_id=1, source_target_pairs={{0,3},{4,7},{8,11},{12,15},{16,19},{20,23},{24,27},{28,31},{1,0},{... | collective-permute-start | bytes 393224 | tf_op jit(solution)/shard_map/ppermute | solution.py:51
  82.9 4.0 %collective-permute-done.19 = bf16[256,256]{1,0:T(8,128)(2,1)S(1)} collective-permute-done((bf16[256,256]{1,0:T(8,128)(2,1)S(1)}, bf16[256,256]{1,0:T(8,128)(2,1)S(1)}, u32[]{:S(2)}, u32[]{:S(2)}) %collective-permute-start.19) | collective-permute-done | bytes 131104 | tf_op jit(solution)/shard_map/ppermute | solution.py:51
  88.3 9.0 %collective-permute-start.22 = (bf16[4,256,256]{2,1,0:T(8,128)(2,1)S(1)}, bf16[4,256,256]{2,1,0:T(8,128)(2,1)S(1)}, u32[]{:S(2)}, u32[]{:S(2)}) collective-permute-start(bf16[4,256,256]{2,1,0:T(8,128)(2,1)S(1)} %pad_maximum_fusion.refs_0_), channel_id=1, source_target_pairs={{0,192},{4,196},{8,200},{12,204},{16,208},{20,212},{24,216},{28,22... | collective-permute-start | bytes 1572872 | tf_op jit(solution)/shard_map/ppermute | solution.py:57
  97.4 4.6 %collective-permute-start.21 = (bf16[4,256,256]{2,1,0:T(8,128)(2,1)S(1)}, bf16[4,256,256]{2,1,0:T(8,128)(2,1)S(1)}, u32[]{:S(2)}, u32[]{:S(2)}) collective-permute-start(bf16[4,256,256]{2,1,0:T(8,128)(2,1)S(1)} %pad_maximum_fusion.refs_0_), channel_id=1, source_target_pairs={{0,128},{4,132},{8,136},{12,140},{16,144},{20,148},{24,152},{28,15... | collective-permute-start | bytes 1572872 | tf_op jit(solution)/shard_map/ppermute | solution.py:57
  102.2 7.4 %collective-permute-done.22.refs_0_ = bf16[4,256,256]{2,1,0:T(8,128)(2,1)S(1)} collective-permute-done((bf16[4,256,256]{2,1,0:T(8,128)(2,1)S(1)}, bf16[4,256,256]{2,1,0:T(8,128)(2,1)S(1)}, u32[]{:S(2)}, u32[]{:S(2)}) %collective-permute-start.22) | collective-permute-done | bytes 524320 | tf_op jit(solution)/shard_map/ppermute | solution.py:57
  110.2 4.5 %collective-permute-done.21.refs_0_ = bf16[4,256,256]{2,1,0:T(8,128)(2,1)S(1)} collective-permute-done((bf16[4,256,256]{2,1,0:T(8,128)(2,1)S(1)}, bf16[4,256,256]{2,1,0:T(8,128)(2,1)S(1)}, u32[]{:S(2)}, u32[]{:S(2)}) %collective-permute-start.21) | collective-permute-done | bytes 524320 | tf_op jit(solution)/shard_map/ppermute | solution.py:57
  116.5 1.9 %shard_map.134 = bf16[128,1024]{1,0:T(8,128)(2,1)} custom-call(f32[128,256]{1,0:T(8,128)S(1)} %get-tuple-element.80.mine, f32[128,256]{1,0:T(8,128)S(1)} %collective-permute-done.24.theirs, bf16[128,1024]{1,0:T(8,128)(2,1)S(1)} %bitcast.51, f32[128,8]{1,0:T(8,128)S(1)} %bitcast.53, f32[128,8]{1,0:T(8,128)S(1)} %bitcast.55, f32[1024,128]{1,0:T(8,128)S(1)} %bitcast.48), custom_call_target="tpu_custom_call" | custom-call | bytes 1048576 | tf_op jit(solution)/shard_map/pallas_call | solution.py:74
  (62 shorter events, 19.7 us)
Async XLA Ops:
  0.6 10.2 %copy-start = (bf16[640,1024]{1,0:T(8,128)(2,1)S(1)}, bf16[640,1024]{1,0:T(8,128)(2,1)}, u32[]{:S(2)}) copy-start(bf16[640,1024]{1,0:T(8,128)(2,1)} %refs_1_.9) | copy-start | bytes 3932164
  0.6 10.2 %collective-permute-start = (bf16[640,1024]{1,0:T(8,128)(2,1)}, bf16[640,1024]{1,0:T(8,128)(2,1)S(1)}, u32[]{:S(2)}, u32[]{:S(2)}) collective-permute-start(bf16[640,1024]{1,0:T(8,128)(2,1)} %refs_1_.9), channel_id=1, source_target_pairs={{0,32},{4,36},{8,40},{12,44},{16,48},{20,52},{24,56},{28,60},{1,33... | collective-permute-start | bytes 3932168 | tf_op jit(solution)/shard_map/ppermute | solution.py:43
  0.7 3.5 %collective-permute-start.5 = (bf16[640,256]{1,0:T(8,128)(2,1)}, bf16[640,256]{1,0:T(8,128)(2,1)}, u32[]{:S(2)}, u32[]{:S(2)}) collective-permute-start(bf16[640,256]{1,0:T(8,128)(2,1)} %refs_3_.1), channel_id=1, source_target_pairs={{0,32},{4,36},{8,40},{12,44},{16,48},{20,52},{24,56},{28,60},{1,33... | collective-permute-start | bytes 983048 | tf_op jit(solution)/shard_map/ppermute | solution.py:43
  1.2 7.4 %collective-permute-start.1 = (bf16[640,256]{1,0:T(8,128)(2,1)}, bf16[640,256]{1,0:T(8,128)(2,1)S(1)}, u32[]{:S(2)}, u32[]{:S(2)}) collective-permute-start(bf16[640,256]{1,0:T(8,128)(2,1)} %refs_3_.1), channel_id=1, source_target_pairs={{0,4},{4,8},{8,12},{12,16},{16,20},{20,24},{24,28},{28,0},{1,5},{5... | collective-permute-start | bytes 983048 | tf_op jit(solution)/shard_map/ppermute | solution.py:47
  4.2 8.6 %collective-permute-start.6 = (bf16[640,256]{1,0:T(8,128)(2,1)}, bf16[640,256]{1,0:T(8,128)(2,1)S(1)}, u32[]{:S(2)}, u32[]{:S(2)}) collective-permute-start(bf16[640,256]{1,0:T(8,128)(2,1)} %collective-permute-done.5.refs_4_), channel_id=1, source_target_pairs={{0,4},{4,8},{8,12},{12,16},{16,20},{20,24},{24,28},{28,0},{1,5},{5... | collective-permute-start | bytes 983048 | tf_op jit(solution)/shard_map/ppermute | solution.py:47
  8.6 8.9 %collective-permute-start.2 = (bf16[640,256]{1,0:T(8,128)(2,1)S(1)}, bf16[640,256]{1,0:T(8,128)(2,1)S(1)}, u32[]{:S(2)}, u32[]{:S(2)}) collective-permute-start(bf16[640,256]{1,0:T(8,128)(2,1)S(1)} %collective-permute-done.1.refs_3_), channel_id=1, source_target_pairs={{0,4},{4,8},{8,12},{12,16},{16,20},{20,24},{24,28},{28,0},{1,5},{5... | collective-permute-start | bytes 983048 | tf_op jit(solution)/shard_map/ppermute | solution.py:47
  12.8 8.2 %collective-permute-start.7 = (bf16[640,256]{1,0:T(8,128)(2,1)S(1)}, bf16[640,256]{1,0:T(8,128)(2,1)S(1)}, u32[]{:S(2)}, u32[]{:S(2)}) collective-permute-start(bf16[640,256]{1,0:T(8,128)(2,1)S(1)} %shard_map.122.refs_4_), channel_id=1, source_target_pairs={{0,4},{4,8},{8,12},{12,16},{16,20},{20,24},{24,28},{28,0},{1,5},{5... | collective-permute-start | bytes 983048 | tf_op jit(solution)/shard_map/ppermute | solution.py:47
  17.5 8.3 %collective-permute-start.3 = (bf16[640,256]{1,0:T(8,128)(2,1)S(1)}, bf16[640,256]{1,0:T(8,128)(2,1)S(1)}, u32[]{:S(2)}, u32[]{:S(2)}) collective-permute-start(bf16[640,256]{1,0:T(8,128)(2,1)S(1)} %collective-permute-done.2.refs_3_), channel_id=1, source_target_pairs={{0,4},{4,8},{8,12},{12,16},{16,20},{20,24},{24,28},{28,0},{1,5},{5... | collective-permute-start | bytes 983048 | tf_op jit(solution)/shard_map/ppermute | solution.py:47
  21.0 8.3 %collective-permute-start.8 = (bf16[640,256]{1,0:T(8,128)(2,1)S(1)}, bf16[640,256]{1,0:T(8,128)(2,1)S(1)}, u32[]{:S(2)}, u32[]{:S(2)}) collective-permute-start(bf16[640,256]{1,0:T(8,128)(2,1)S(1)} %shard_map.124.refs_4_), channel_id=1, source_target_pairs={{0,4},{4,8},{8,12},{12,16},{16,20},{20,24},{24,28},{28,0},{1,5},{5... | collective-permute-start | bytes 983048 | tf_op jit(solution)/shard_map/ppermute | solution.py:47
  25.8 8.3 %collective-permute-start.4 = (bf16[640,256]{1,0:T(8,128)(2,1)S(1)}, bf16[640,256]{1,0:T(8,128)(2,1)S(1)}, u32[]{:S(2)}, u32[]{:S(2)}) collective-permute-start(bf16[640,256]{1,0:T(8,128)(2,1)S(1)} %collective-permute-done.3.refs_3_), channel_id=1, source_target_pairs={{0,4},{4,8},{8,12},{12,16},{16,20},{20,24},{24,28},{28,0},{1,5},{5... | collective-permute-start | bytes 983048 | tf_op jit(solution)/shard_map/ppermute | solution.py:47
  26.9 4.5 %copy-start.2 = (bf16[4,32,1024]{2,1,0:T(8,128)(2,1)S(1)}, bf16[4,32,1024]{2,1,0:T(8,128)(2,1)}, u32[]{:S(2)}) copy-start(bf16[4,32,1024]{2,1,0:T(8,128)(2,1)} %param.15) | copy-start | bytes 786436
  26.9 4.6 %copy-start.8 = (s32[32]{0:T(128)S(1)}, s32[32]{0:T(128)}, u32[]{:S(2)}) copy-start(s32[32]{0:T(128)} %param.17) | copy-start | bytes 388
  29.3 8.3 %collective-permute-start.9 = (bf16[640,256]{1,0:T(8,128)(2,1)S(1)}, bf16[640,256]{1,0:T(8,128)(2,1)S(1)}, u32[]{:S(2)}, u32[]{:S(2)}) collective-permute-start(bf16[640,256]{1,0:T(8,128)(2,1)S(1)} %shard_map.126.refs_4_), channel_id=1, source_target_pairs={{0,4},{4,8},{8,12},{12,16},{16,20},{20,24},{24,28},{28,0},{1,5},{5... | collective-permute-start | bytes 983048 | tf_op jit(solution)/shard_map/ppermute | solution.py:47
  37.6 6.8 %copy-start.7 = (bf16[32,256,256]{2,1,0:T(8,128)(2,1)S(1)}, bf16[32,256,256]{2,1,0:T(8,128)(2,1)}, u32[]{:S(2)}) copy-start(bf16[32,256,256]{2,1,0:T(8,128)(2,1)} %param.16) | copy-start | bytes 12582916
  38.8 10.4 %collective-permute-start.10 = (bf16[4,256,256]{2,1,0:T(8,128)(2,1)S(1)}, bf16[4,256,256]{2,1,0:T(8,128)(2,1)S(1)}, u32[]{:S(2)}, u32[]{:S(2)}) collective-permute-start(bf16[4,256,256]{2,1,0:T(8,128)(2,1)S(1)} %get-tuple-element.64), channel_id=1, source_target_pairs={{0,1},{4,5},{8,9},{12,13},{16,17},{20,21},{24,25},{28,29},{1,2},{5... | collective-permute-start | bytes 1572872 | tf_op jit(solution)/shard_map/ppermute | solution.py:51
  40.3 15.5 %collective-permute-start.11 = (bf16[4,256,256]{2,1,0:T(8,128)(2,1)S(1)}, bf16[4,256,256]{2,1,0:T(8,128)(2,1)S(1)}, u32[]{:S(2)}, u32[]{:S(2)}) collective-permute-start(bf16[4,256,256]{2,1,0:T(8,128)(2,1)S(1)} %get-tuple-element.65), channel_id=1, source_target_pairs={{0,2},{4,6},{8,10},{12,14},{16,18},{20,22},{24,26},{28,30},{1,3},{... | collective-permute-start | bytes 1572872 | tf_op jit(solution)/shard_map/ppermute | solution.py:51
  43.0 12.8 %collective-permute-start.12 = (bf16[4,256,256]{2,1,0:T(8,128)(2,1)S(1)}, bf16[4,256,256]{2,1,0:T(8,128)(2,1)S(1)}, u32[]{:S(2)}, u32[]{:S(2)}) collective-permute-start(bf16[4,256,256]{2,1,0:T(8,128)(2,1)S(1)} %get-tuple-element.66), channel_id=1, source_target_pairs={{0,3},{4,7},{8,11},{12,15},{16,19},{20,23},{24,27},{28,31},{1,0},{... | collective-permute-start | bytes 1572872 | tf_op jit(solution)/shard_map/ppermute | solution.py:51
  55.8 21.0 %copy-start.4 = (f32[256,256]{1,0:T(8,128)S(1)}, f32[256,256]{1,0:T(8,128)}, u32[]{:S(2)}) copy-start(f32[256,256]{1,0:T(8,128)} %master.1) | copy-start | bytes 786436
  55.8 21.0 %copy-start.5 = (bf16[256,256]{1,0:T(8,128)(2,1)S(1)}, bf16[256,256]{1,0:T(8,128)(2,1)}, u32[]{:S(2)}) copy-start(bf16[256,256]{1,0:T(8,128)(2,1)} %first_moment.1) | copy-start | bytes 393220
  55.8 21.0 %copy-start.6 = (bf16[256,256]{1,0:T(8,128)(2,1)S(1)}, bf16[256,256]{1,0:T(8,128)(2,1)}, u32[]{:S(2)}) copy-start(bf16[256,256]{1,0:T(8,128)(2,1)} %second_moment.1) | copy-start | bytes 393220
  56.6 7.7 %collective-permute-start.13 = (f32[256,256]{1,0:T(8,128)S(1)}, f32[256,256]{1,0:T(8,128)S(1)}, u32[]{:S(2)}, u32[]{:S(2)}) collective-permute-start(f32[256,256]{1,0:T(8,128)S(1)} %get-tuple-element.68), channel_id=1, source_target_pairs={{0,64},{4,68},{8,72},{12,76},{16,80},{20,84},{24,88},{28,92},{1,65... | collective-permute-start | bytes 786440 | tf_op jit(solution)/shard_map/ppermute | solution.py:57
  58.2 10.1 %collective-permute-start.14 = (f32[256,256]{1,0:T(8,128)S(1)}, f32[256,256]{1,0:T(8,128)S(1)}, u32[]{:S(2)}, u32[]{:S(2)}) collective-permute-start(f32[256,256]{1,0:T(8,128)S(1)} %get-tuple-element.69), channel_id=1, source_target_pairs={{0,128},{4,132},{8,136},{12,140},{16,144},{20,148},{24,152},{28,15... | collective-permute-start | bytes 786440 | tf_op jit(solution)/shard_map/ppermute | solution.py:57
  61.1 7.2 %collective-permute-start.15 = (f32[256,256]{1,0:T(8,128)S(1)}, f32[256,256]{1,0:T(8,128)S(1)}, u32[]{:S(2)}, u32[]{:S(2)}) collective-permute-start(f32[256,256]{1,0:T(8,128)S(1)} %get-tuple-element.70), channel_id=1, source_target_pairs={{0,192},{4,196},{8,200},{12,204},{16,208},{20,212},{24,216},{28,22... | collective-permute-start | bytes 786440 | tf_op jit(solution)/shard_map/ppermute | solution.py:57
  62.5 39.4 %collective-permute-start.17 = (bf16[16,128,256]{2,1,0:T(8,128)(2,1)S(1)}, bf16[16,128,256]{2,1,0:T(8,128)(2,1)S(1)}, u32[]{:S(2)}, u32[]{:S(2)}) collective-permute-start(bf16[16,128,256]{2,1,0:T(8,128)(2,1)S(1)} %get-tuple-element.74), channel_id=1, source_target_pairs={{0,32},{4,36},{8,40},{12,44},{16,48},{20,52},{24,56},{28,60},{1,33... | collective-permute-start | bytes 3145736 | tf_op jit(solution)/shard_map/ppermute | solution.py:43
  68.4 8.4 %collective-permute-start.16 = (bf16[256,256]{1,0:T(8,128)(2,1)S(1)}, bf16[256,256]{1,0:T(8,128)(2,1)S(1)}, u32[]{:S(2)}, u32[]{:S(2)}) collective-permute-start(bf16[256,256]{1,0:T(8,128)(2,1)S(1)} %add_convert_fusion), channel_id=1, source_target_pairs={{0,0},{4,36},{8,72},{12,108},{16,144},{20,180},{24,216},{28,252},{... | collective-permute-start | bytes 393224 | tf_op jit(solution)/shard_map/ppermute | solution.py:63
  77.9 5.1 %collective-permute-start.18 = (bf16[256,256]{1,0:T(8,128)(2,1)S(1)}, bf16[256,256]{1,0:T(8,128)(2,1)S(1)}, u32[]{:S(2)}, u32[]{:S(2)}) collective-permute-start(bf16[256,256]{1,0:T(8,128)(2,1)S(1)} %get-tuple-element.75), channel_id=1, source_target_pairs={{0,3},{4,7},{8,11},{12,15},{16,19},{20,23},{24,27},{28,31},{1,0},{... | collective-permute-start | bytes 393224 | tf_op jit(solution)/shard_map/ppermute | solution.py:51
  80.4 6.5 %collective-permute-start.19 = (bf16[256,256]{1,0:T(8,128)(2,1)S(1)}, bf16[256,256]{1,0:T(8,128)(2,1)S(1)}, u32[]{:S(2)}, u32[]{:S(2)}) collective-permute-start(bf16[256,256]{1,0:T(8,128)(2,1)S(1)} %get-tuple-element.75), channel_id=1, source_target_pairs={{0,2},{4,6},{8,10},{12,14},{16,18},{20,22},{24,26},{28,30},{1,3},{... | collective-permute-start | bytes 393224 | tf_op jit(solution)/shard_map/ppermute | solution.py:51
  81.8 6.5 %collective-permute-start.20 = (bf16[256,256]{1,0:T(8,128)(2,1)S(1)}, bf16[256,256]{1,0:T(8,128)(2,1)S(1)}, u32[]{:S(2)}, u32[]{:S(2)}) collective-permute-start(bf16[256,256]{1,0:T(8,128)(2,1)S(1)} %get-tuple-element.75), channel_id=1, source_target_pairs={{0,1},{4,5},{8,9},{12,13},{16,17},{20,21},{24,25},{28,29},{1,2},{5... | collective-permute-start | bytes 393224 | tf_op jit(solution)/shard_map/ppermute | solution.py:51
  88.3 21.4 %collective-permute-start.22 = (bf16[4,256,256]{2,1,0:T(8,128)(2,1)S(1)}, bf16[4,256,256]{2,1,0:T(8,128)(2,1)S(1)}, u32[]{:S(2)}, u32[]{:S(2)}) collective-permute-start(bf16[4,256,256]{2,1,0:T(8,128)(2,1)S(1)} %pad_maximum_fusion.refs_0_), channel_id=1, source_target_pairs={{0,192},{4,196},{8,200},{12,204},{16,208},{20,212},{24,216},{28,22... | collective-permute-start | bytes 1572872 | tf_op jit(solution)/shard_map/ppermute | solution.py:57
  97.4 12.3 %collective-permute-start.23 = (bf16[4,256,256]{2,1,0:T(8,128)(2,1)S(1)}, bf16[4,256,256]{2,1,0:T(8,128)(2,1)S(1)}, u32[]{:S(2)}, u32[]{:S(2)}) collective-permute-start(bf16[4,256,256]{2,1,0:T(8,128)(2,1)S(1)} %pad_maximum_fusion.refs_0_), channel_id=1, source_target_pairs={{0,64},{4,68},{8,72},{12,76},{16,80},{20,84},{24,88},{28,92},{1,65... | collective-permute-start | bytes 1572872 | tf_op jit(solution)/shard_map/ppermute | solution.py:57
  97.4 17.3 %collective-permute-start.21 = (bf16[4,256,256]{2,1,0:T(8,128)(2,1)S(1)}, bf16[4,256,256]{2,1,0:T(8,128)(2,1)S(1)}, u32[]{:S(2)}, u32[]{:S(2)}) collective-permute-start(bf16[4,256,256]{2,1,0:T(8,128)(2,1)S(1)} %pad_maximum_fusion.refs_0_), channel_id=1, source_target_pairs={{0,128},{4,132},{8,136},{12,140},{16,144},{20,148},{24,152},{28,15... | collective-permute-start | bytes 1572872 | tf_op jit(solution)/shard_map/ppermute | solution.py:57
  115.0 1.4 %collective-permute-start.24 = (f32[128,256]{1,0:T(8,128)S(1)}, f32[128,256]{1,0:T(8,128)S(1)}, u32[]{:S(2)}, u32[]{:S(2)}) collective-permute-start(f32[128,256]{1,0:T(8,128)S(1)} %get-tuple-element.81), channel_id=1, source_target_pairs={{0,32},{4,36},{8,40},{12,44},{16,48},{20,52},{24,56},{28,60},{1,33... | collective-permute-start | bytes 393224 | tf_op jit(solution)/shard_map/ppermute | solution.py:43
  (2 other events, 4.6 us)
